TPU v7x, 32 devices: a whole 2x2x4 slice. The times are simulated.
32 devices in a mesh: dp: 8 (over z, y), mp: 4 (over x, core).
Axes of the slice: x: 2, y: 2, z: 4, core: 2. Of those that a mesh axis runs over, the one named last changes fastest.
Arguments:
- tokens_in: bfloat16 [4096, 1024], P('dp'), may hold values from -6 to 6
- masked_positions: int32 [8, 96], P('dp'), may hold values from 0 to 512, as said below
- replace_choice: int32 [8, 96], P('dp'), may hold values from 0 to 33
- replace_table: bfloat16 [34, 1024], replicated, may hold values from -6 to 6
- masked_cotangent: bfloat16 [8, 96, 1024], P('dp'), may hold values from -6 to 6
- attend: float32 [1024, 3, 1024], P('dp', None, 'mp'), may hold values from -0.1875 to 0.1875
- attend_mean: float32 [1024, 3, 1024], P('dp', None, 'mp'), may hold values from -1 to 1
- attend_square: float32 [1024, 3, 1024], P('dp', None, 'mp'), may hold values from 0.004096 to 0.016384
- attend_shadow: float32 [1024, 3, 1024], P('dp', None, 'mp'), may hold values from -0.0009765625 to 0.0009765625
- rejoin: float32 [1024, 1024], P('dp', 'mp'), may hold values from -0.75 to 0.75
- rejoin_mean: float32 [1024, 1024], P('dp', 'mp'), may hold values from -1 to 1
- rejoin_square: float32 [1024, 1024], P('dp', 'mp'), may hold values from 0.004096 to 0.016384
- rejoin_shadow: float32 [1024, 1024], P('dp', 'mp'), may hold values from -0.00390625 to 0.00390625
- expand: float32 [1024, 4096], P('dp', 'mp'), may hold values from -0.1875 to 0.1875
- expand_mean: float32 [1024, 4096], P('dp', 'mp'), may hold values from -1 to 1
- expand_square: float32 [1024, 4096], P('dp', 'mp'), may hold values from 0.004096 to 0.016384
- expand_shadow: float32 [1024, 4096], P('dp', 'mp'), may hold values from -0.0009765625 to 0.0009765625
- narrow: float32 [1024, 4096], P('dp', 'mp'), may hold values from -0.09375 to 0.09375
- narrow_mean: float32 [1024, 4096], P('dp', 'mp'), may hold values from -1 to 1
- narrow_square: float32 [1024, 4096], P('dp', 'mp'), may hold values from 0.004096 to 0.016384
- narrow_shadow: float32 [1024, 4096], P('dp', 'mp'), may hold values from -0.00048828125 to 0.00048828125
- vectors: float32 [1024, 12], P('dp', 'mp')
- vectors_mean: float32 [1024, 12], P('dp', 'mp'), may hold values from -3 to 3
- vectors_square: float32 [1024, 12], P('dp', 'mp'), may hold values from 0.036864 to 0.147456
- vectors_shadow: float32 [1024, 12], P('dp', 'mp'), may hold values from -0.0234375 to 0.0234375
Outputs:
- activations: float32 [4096, 1024], P('dp')
- input_gradient: float32 [4096, 1024], P('dp')
- gradient_norm: float32 [], replicated
- next_attend: float32 [1024, 3, 1024], P('dp', None, 'mp')
- momentum_attend: float32 [1024, 3, 1024], P('dp', None, 'mp')
- variance_attend: float32 [1024, 3, 1024], P('dp', None, 'mp')
- average_attend: float32 [1024, 3, 1024], P('dp', None, 'mp')
- copy_attend: bfloat16 [1024, 3, 1024], P('dp', None, 'mp')
- next_rejoin: float32 [1024, 1024], P('dp', 'mp')
- momentum_rejoin: float32 [1024, 1024], P('dp', 'mp')
- variance_rejoin: float32 [1024, 1024], P('dp', 'mp')
- average_rejoin: float32 [1024, 1024], P('dp', 'mp')
- copy_rejoin: bfloat16 [1024, 1024], P('dp', 'mp')
- next_expand: float32 [1024, 4096], P('dp', 'mp')
- momentum_expand: float32 [1024, 4096], P('dp', 'mp')
- variance_expand: float32 [1024, 4096], P('dp', 'mp')
- average_expand: float32 [1024, 4096], P('dp', 'mp')
- copy_expand: bfloat16 [1024, 4096], P('dp', 'mp')
- next_narrow: float32 [1024, 4096], P('dp', 'mp')
- momentum_narrow: float32 [1024, 4096], P('dp', 'mp')
- variance_narrow: float32 [1024, 4096], P('dp', 'mp')
- average_narrow: float32 [1024, 4096], P('dp', 'mp')
- copy_narrow: bfloat16 [1024, 4096], P('dp', 'mp')
- next_vectors: float32 [1024, 12], P('dp', 'mp')
- momentum_vectors: float32 [1024, 12], P('dp', 'mp')
- variance_vectors: float32 [1024, 12], P('dp', 'mp')
- average_vectors: float32 [1024, 12], P('dp', 'mp')
- copy_vectors: bfloat16 [1024, 12], P('dp', 'mp')
Inputs may be any that keep to these rules, and one draw needn't show every extreme that they name: `masked_positions`: row s lists the masked positions of sequence s: its first entries are distinct positions below 512, the remaining entries equal 512 and mark empty slots. Each row has 48 to 96 positions; some row has 96 and some row 48.
All inputs are finite; a program needn't handle non-finite values.
Results may differ from a plain program's by a relative error of at most 0.035.
Values may be sent and summed in bfloat16 or wider, within the bound.
A program may use at most 128 MiB of HBM per device.

v0:
```python
import math

import jax
import jax.numpy as jnp
from jax import lax
from jax.sharding import PartitionSpec as P

D = 1024
HEAD_DIM = 64
FF = 4096
SEQ_LEN = 512
DEPTH = 2
STEP = 7


norm_eps = 1e-05


def layer_norm(tensor, norm_gain, norm_shift):
    centred = tensor - jnp.mean(tensor, axis=-1, keepdims=True)
    spread = lax.rsqrt(jnp.mean(centred * centred, axis=-1, keepdims=True) + norm_eps)
    return centred * spread * norm_gain + norm_shift


def activate(tensor):
    return jax.nn.gelu(tensor, approximate=True)


def product(former, latter):
    return jnp.dot(former, latter, preferred_element_type=jnp.float32)


def over_rows(former, latter):
    return lax.dot_general(
        former, latter, (((0,), (0,)), ((), ())), preferred_element_type=jnp.float32
    )


def over_columns(former, latter):
    return lax.dot_general(
        former, latter, (((1,), (1,)), ((), ())), preferred_element_type=jnp.float32
    )


def split_heads(segment):
    return segment.reshape(segment.shape[0], segment.shape[1] // HEAD_DIM, HEAD_DIM)


def attention_forward(segment):
    queries, key_rows, value_rows = segment
    scaling = HEAD_DIM ** (-0.5)
    scores = (
        jnp.einsum(
            "qhd,khd->hqk",
            split_heads(queries),
            split_heads(key_rows),
            preferred_element_type=jnp.float32,
        )
        * scaling
    )
    peak_score = jnp.max(scores, axis=-1, keepdims=True)
    raised = jnp.exp(scores - peak_score)
    row_total = jnp.sum(raised, axis=-1, keepdims=True)
    shares = (raised / row_total).astype(jnp.bfloat16)
    context = jnp.einsum(
        "hqk,khd->qhd", shares, split_heads(value_rows), preferred_element_type=jnp.float32
    )
    return (
        context.reshape(queries.shape).astype(jnp.bfloat16),
        peak_score[:, :, 0],
        row_total[:, :, 0],
    )


def attention_backward(segment):
    queries, key_rows, value_rows, peak_score, row_total, back_context = segment
    scaling = HEAD_DIM ** (-0.5)
    query_heads = split_heads(queries)
    key_heads = split_heads(key_rows)
    back_heads = split_heads(back_context)
    scores = (
        jnp.einsum("qhd,khd->hqk", query_heads, key_heads, preferred_element_type=jnp.float32)
        * scaling
    )
    shares = jnp.exp(scores - peak_score[:, :, None]) / row_total[:, :, None]
    back_value = jnp.einsum(
        "hqk,qhd->khd", shares.astype(jnp.bfloat16), back_heads, preferred_element_type=jnp.float32
    )
    back_shares = jnp.einsum(
        "qhd,khd->hqk", back_heads, split_heads(value_rows), preferred_element_type=jnp.float32
    )
    row_inner = jnp.sum(shares * back_shares, axis=-1, keepdims=True)
    back_scores = (shares * (back_shares - row_inner)).astype(jnp.bfloat16)
    back_query = (
        jnp.einsum("hqk,khd->qhd", back_scores, key_heads, preferred_element_type=jnp.float32)
        * scaling
    )
    back_key = (
        jnp.einsum("hqk,qhd->khd", back_scores, query_heads, preferred_element_type=jnp.float32)
        * scaling
    )
    row_shape = queries.shape
    return (
        back_query.reshape(row_shape),
        back_key.reshape(row_shape),
        back_value.reshape(row_shape),
    )


def forward_step(stream, gathered, vector_table, model_index):
    attend_full, rejoin_full, expand_full, narrow_full = gathered
    features = stream.shape[1]
    head_width = attend_full.shape[2]
    unit_width = expand_full.shape[1]
    query_bias = lax.dynamic_slice_in_dim(vector_table[:, 0], model_index * head_width, head_width)
    value_bias = lax.dynamic_slice_in_dim(vector_table[:, 1], model_index * head_width, head_width)
    unit_bias = lax.dynamic_slice_in_dim(
        vector_table[:, 8:12].T.reshape(4 * features), model_index * unit_width, unit_width
    )
    lowered = stream.astype(jnp.bfloat16)
    projected = product(lowered, attend_full.reshape(features, 3 * head_width))
    queries = (projected[:, :head_width] + query_bias).astype(jnp.bfloat16)
    key_rows = projected[:, head_width : 2 * head_width].astype(jnp.bfloat16)
    value_rows = (projected[:, 2 * head_width :] + value_bias).astype(jnp.bfloat16)
    sequences = stream.shape[0] // SEQ_LEN
    row_shape = (sequences, SEQ_LEN, head_width)
    context, peak_score, row_total = lax.map(
        attention_forward,
        (queries.reshape(row_shape), key_rows.reshape(row_shape), value_rows.reshape(row_shape)),
    )
    context = context.reshape(stream.shape[0], head_width)
    mixed_sum = lax.psum(over_columns(context, rejoin_full).astype(jnp.bfloat16), "mp").astype(
        jnp.float32
    )
    residual_one = stream + (mixed_sum + vector_table[:, 2])
    normed = layer_norm(residual_one, vector_table[:, 4], vector_table[:, 5])
    expanded = product(normed.astype(jnp.bfloat16), expand_full) + unit_bias
    active = activate(expanded).astype(jnp.bfloat16)
    reduced = lax.psum(over_columns(active, narrow_full).astype(jnp.bfloat16), "mp").astype(
        jnp.float32
    )
    residual_two = normed + (reduced + vector_table[:, 3])
    output = layer_norm(residual_two, vector_table[:, 6], vector_table[:, 7])
    saved_state = (
        stream,
        queries,
        key_rows,
        value_rows,
        peak_score,
        row_total,
        context,
        residual_one,
        normed,
        expanded,
        residual_two,
    )
    return (output, saved_state)


def backward_step(back_out, saved_state, gathered, vector_table, model_index):
    (
        stream,
        queries,
        key_rows,
        value_rows,
        peak_score,
        row_total,
        context,
        residual_one,
        normed,
        expanded,
        residual_two,
    ) = saved_state
    attend_full, rejoin_full, expand_full, narrow_full = gathered
    features = stream.shape[1]
    head_width = attend_full.shape[2]
    unit_width = expand_full.shape[1]
    norm_value, norm_pull = jax.vjp(
        layer_norm, residual_two, vector_table[:, 6], vector_table[:, 7]
    )
    back_two, back_gain_two, back_shift_two = norm_pull(back_out)
    low_two = back_two.astype(jnp.bfloat16)
    active_full, active_pull = jax.vjp(activate, expanded)
    back_narrow = over_rows(low_two, active_full.astype(jnp.bfloat16))
    back_active = product(low_two, narrow_full)
    back_expanded = active_pull(back_active)[0].astype(jnp.bfloat16)
    back_expand = over_rows(normed.astype(jnp.bfloat16), back_expanded)
    back_unit_bias = jnp.sum(back_expanded.astype(jnp.float32), axis=0)
    back_normed = back_two + lax.psum(
        over_columns(back_expanded, expand_full).astype(jnp.bfloat16), "mp"
    ).astype(jnp.float32)
    first_value, first_pull = jax.vjp(
        layer_norm, residual_one, vector_table[:, 4], vector_table[:, 5]
    )
    back_one, back_gain_one, back_shift_one = first_pull(back_normed)
    low_one = back_one.astype(jnp.bfloat16)
    back_rejoin = over_rows(low_one, context)
    back_context = product(low_one, rejoin_full).astype(jnp.bfloat16)
    sequences = stream.shape[0] // SEQ_LEN
    row_shape = (sequences, SEQ_LEN, head_width)
    back_query, back_key, back_value = lax.map(
        attention_backward,
        (
            queries.reshape(row_shape),
            key_rows.reshape(row_shape),
            value_rows.reshape(row_shape),
            peak_score,
            row_total,
            back_context.reshape(row_shape),
        ),
    )
    back_projected = jnp.concatenate(
        [
            back_query.reshape(-1, head_width),
            back_key.reshape(-1, head_width),
            back_value.reshape(-1, head_width),
        ],
        axis=1,
    ).astype(jnp.bfloat16)
    back_attend = over_rows(stream.astype(jnp.bfloat16), back_projected).reshape(
        features, 3, head_width
    )
    back_stream = back_one + lax.psum(
        over_columns(back_projected, attend_full.reshape(features, 3 * head_width)).astype(
            jnp.bfloat16
        ),
        "mp",
    ).astype(jnp.float32)
    back_query_bias = jnp.sum(back_projected[:, :head_width].astype(jnp.float32), axis=0)
    back_value_bias = jnp.sum(back_projected[:, 2 * head_width :].astype(jnp.float32), axis=0)
    owner_flag = (model_index == 0).astype(jnp.float32)
    shared = (
        jnp.stack(
            [
                jnp.sum(back_one, axis=0),
                jnp.sum(back_two, axis=0),
                back_gain_one,
                back_shift_one,
                back_gain_two,
                back_shift_two,
            ],
            axis=1,
        )
        * owner_flag
    )
    query_column = lax.dynamic_update_slice_in_dim(
        jnp.zeros((features,), jnp.float32), back_query_bias, model_index * head_width, 0
    )
    value_column = lax.dynamic_update_slice_in_dim(
        jnp.zeros((features,), jnp.float32), back_value_bias, model_index * head_width, 0
    )
    unit_columns = (
        lax.dynamic_update_slice_in_dim(
            jnp.zeros((4 * features,), jnp.float32), back_unit_bias, model_index * unit_width, 0
        )
        .reshape(4, features)
        .T
    )
    back_vectors = jnp.concatenate(
        [query_column[:, None], value_column[:, None], shared, unit_columns], axis=1
    )
    return (back_stream, (back_attend, back_rejoin, back_expand, back_narrow), back_vectors)


def apply_update(weight, first_moment, second_moment, shadow, gradient, step_rate):
    momentum = 0.5 * first_moment + 0.5 * gradient
    variance = 0.5 * second_moment + 0.5 * gradient * gradient
    bias_fix = 1.0 - 0.5**STEP
    updated = weight - step_rate * (
        momentum / bias_fix / (jnp.sqrt(variance / bias_fix) + 1e-08) + 0.01 * weight
    )
    average = 0.999 * shadow + 0.001 * updated
    return (updated, momentum, variance, average, updated.astype(jnp.bfloat16))


def per_device(
    tokens_in,
    masked_positions,
    replace_choice,
    replace_table,
    masked_cotangent,
    attend,
    attend_mean,
    attend_square,
    attend_shadow,
    rejoin,
    rejoin_mean,
    rejoin_square,
    rejoin_shadow,
    expand,
    expand_mean,
    expand_square,
    expand_shadow,
    narrow,
    narrow_mean,
    narrow_square,
    narrow_shadow,
    vectors,
    vectors_mean,
    vectors_square,
    vectors_shadow,
):
    data_size = lax.axis_size("dp")
    model_size = lax.axis_size("mp")
    model_index = lax.axis_index("mp")
    sequences = masked_positions.shape[0]
    features = tokens_in.shape[1]
    positions = jnp.arange(SEQ_LEN, dtype=jnp.int32)
    slot_match = (masked_positions[:, :, None] == positions[None, None, :]).astype(jnp.bfloat16)
    masked_flag = jnp.sum(slot_match.astype(jnp.float32), axis=1)
    replace_hot = (
        replace_choice[:, :, None]
        == jnp.arange(replace_table.shape[0], dtype=jnp.int32)[None, None, :]
    ).astype(jnp.bfloat16)
    replacements = jnp.einsum(
        "sjr,rd->sjd", replace_hot, replace_table, preferred_element_type=jnp.float32
    ).astype(jnp.bfloat16)
    placed_rows = jnp.einsum(
        "sjp,sjd->spd", slot_match, replacements, preferred_element_type=jnp.float32
    )
    kept_flag = (1.0 - masked_flag)[:, :, None]
    embedded = (
        tokens_in.astype(jnp.float32).reshape(sequences, SEQ_LEN, features) * kept_flag
        + placed_rows
    )
    cotangent = jnp.einsum(
        "sjp,sjd->spd", slot_match, masked_cotangent, preferred_element_type=jnp.float32
    )
    vector_rows = vectors.shape[0]
    vector_width = vectors.shape[1]
    gathered_vectors = lax.all_gather(
        vectors.astype(jnp.bfloat16).reshape(1, vector_rows * vector_width),
        ("dp", "mp"),
        axis=0,
        tiled=True,
    )
    vector_table = (
        gathered_vectors.reshape(data_size, model_size, vector_rows, vector_width)
        .transpose(0, 2, 1, 3)
        .reshape(data_size * vector_rows, model_size * vector_width)
        .astype(jnp.float32)
    )
    low_attend = attend.astype(jnp.bfloat16)
    low_rejoin = rejoin.astype(jnp.bfloat16)
    low_expand = expand.astype(jnp.bfloat16)
    low_narrow = narrow.astype(jnp.bfloat16)
    stream = embedded.reshape(-1, features)
    saved_states = []
    for depth_index in range(DEPTH):
        gathered = (
            lax.all_gather(low_attend, "dp", axis=0, tiled=True),
            lax.all_gather(low_rejoin, "dp", axis=0, tiled=True),
            lax.all_gather(low_expand, "dp", axis=0, tiled=True),
            lax.all_gather(low_narrow, "dp", axis=0, tiled=True),
        )
        stream, saved_state = forward_step(stream, gathered, vector_table, model_index)
        saved_states.append(saved_state)
    stream_back = cotangent.reshape(-1, features)
    for depth_index in reversed(range(DEPTH)):
        gathered = (
            lax.all_gather(low_attend, "dp", axis=0, tiled=True),
            lax.all_gather(low_rejoin, "dp", axis=0, tiled=True),
            lax.all_gather(low_expand, "dp", axis=0, tiled=True),
            lax.all_gather(low_narrow, "dp", axis=0, tiled=True),
        )
        stream_back, matrix_back, vector_back = backward_step(
            stream_back, saved_states[depth_index], gathered, vector_table, model_index
        )
        if depth_index == DEPTH - 1:
            vector_total = vector_back
        else:
            vector_total = vector_total + vector_back
        reduced_back = (
            lax.psum_scatter(matrix_back[0], "dp", scatter_dimension=0, tiled=True),
            lax.psum_scatter(matrix_back[1], "dp", scatter_dimension=0, tiled=True),
            lax.psum_scatter(matrix_back[2], "dp", scatter_dimension=0, tiled=True),
            lax.psum_scatter(matrix_back[3], "dp", scatter_dimension=0, tiled=True),
        )
        if depth_index == DEPTH - 1:
            shards = reduced_back
        else:
            shards = jax.tree.map(jnp.add, shards, reduced_back)
    vector_terms = (
        vector_total.reshape(data_size, vector_rows, model_size, vector_width)
        .transpose(0, 2, 1, 3)
        .reshape(data_size * model_size, vector_rows * vector_width)
    )
    vector_grads = lax.psum_scatter(
        vector_terms, ("dp", "mp"), scatter_dimension=0, tiled=True
    ).reshape(vector_rows, vector_width)
    local_squares = (
        jnp.sum(shards[0] * shards[0])
        + jnp.sum(shards[1] * shards[1])
        + jnp.sum(shards[2] * shards[2])
        + jnp.sum(shards[3] * shards[3])
        + jnp.sum(vector_grads * vector_grads)
    )
    gradient_norm = jnp.sqrt(lax.psum(local_squares, ("dp", "mp")))
    param_count = 4 * D * D + 2 * D * FF + 12 * D
    clip_limit = 0.001 * math.sqrt(param_count * tokens_in.shape[0] * data_size)
    factor = jnp.minimum(1.0, clip_limit / (gradient_norm + 1e-06))
    attend_out = apply_update(
        attend, attend_mean, attend_square, attend_shadow, shards[0] * factor, 0.04
    )
    rejoin_out = apply_update(
        rejoin, rejoin_mean, rejoin_square, rejoin_shadow, shards[1] * factor, 0.16
    )
    expand_out = apply_update(
        expand, expand_mean, expand_square, expand_shadow, shards[2] * factor, 0.04
    )
    narrow_out = apply_update(
        narrow, narrow_mean, narrow_square, narrow_shadow, shards[3] * factor, 0.04
    )
    vectors_out = apply_update(
        vectors, vectors_mean, vectors_square, vectors_shadow, vector_grads * factor, 0.5
    )
    input_gradient = (stream_back.reshape(sequences, SEQ_LEN, features) * kept_flag).reshape(
        -1, features
    )
    return (
        stream,
        input_gradient,
        gradient_norm,
        attend_out[0],
        attend_out[1],
        attend_out[2],
        attend_out[3],
        attend_out[4],
        rejoin_out[0],
        rejoin_out[1],
        rejoin_out[2],
        rejoin_out[3],
        rejoin_out[4],
        expand_out[0],
        expand_out[1],
        expand_out[2],
        expand_out[3],
        expand_out[4],
        narrow_out[0],
        narrow_out[1],
        narrow_out[2],
        narrow_out[3],
        narrow_out[4],
        vectors_out[0],
        vectors_out[1],
        vectors_out[2],
        vectors_out[3],
        vectors_out[4],
    )


def solution(mesh):
    placed = (
        P("dp", None),
        P("dp", None),
        P("dp", None),
        P(),
        P("dp", None, None),
        P("dp", None, "mp"),
        P("dp", None, "mp"),
        P("dp", None, "mp"),
        P("dp", None, "mp"),
        P("dp", "mp"),
        P("dp", "mp"),
        P("dp", "mp"),
        P("dp", "mp"),
        P("dp", "mp"),
        P("dp", "mp"),
        P("dp", "mp"),
        P("dp", "mp"),
        P("dp", "mp"),
        P("dp", "mp"),
        P("dp", "mp"),
        P("dp", "mp"),
        P("dp", "mp"),
        P("dp", "mp"),
        P("dp", "mp"),
        P("dp", "mp"),
    )
    return jax.shard_map(
        per_device,
        mesh=mesh,
        in_specs=placed,
        out_specs=(
            P("dp", None),
            P("dp", None),
            P(),
            P("dp", None, "mp"),
            P("dp", None, "mp"),
            P("dp", None, "mp"),
            P("dp", None, "mp"),
            P("dp", None, "mp"),
            P("dp", "mp"),
            P("dp", "mp"),
            P("dp", "mp"),
            P("dp", "mp"),
            P("dp", "mp"),
            P("dp", "mp"),
            P("dp", "mp"),
            P("dp", "mp"),
            P("dp", "mp"),
            P("dp", "mp"),
            P("dp", "mp"),
            P("dp", "mp"),
            P("dp", "mp"),
            P("dp", "mp"),
            P("dp", "mp"),
            P("dp", "mp"),
            P("dp", "mp"),
            P("dp", "mp"),
            P("dp", "mp"),
            P("dp", "mp"),
        ),
        check_vma=False,
    )
```

profile of v0, /device:TPU:0, one launch (start us, length us, event | category | flops | bytes accessed | tf_op | source)
XLA Modules:
  0.0 972.5 jit_solution(9359548180218591491)
XLA Ops:
  10.2 43.7 %all-gather = bf16[32,1,384]{2,1,0:T(2,128)(2,1)S(1)} all-gather(bf16[1,1,384]{2,1,0:T(2,128)(2,1)S(1)} %reshape.592), channel_id=1, replica_groups=mesh['dp'=8,'mp'=4] {'dp','mp'}, dimensions={0}, use_global_device_ids=true | all-gather | bytes 25344 | tf_op jit(solution)/shard_map/all_gather | solution.py:331
  55.9 31.2 %all_gather.12 = bf16[1024,256]{1,0:T(8,128)(2,1)S(1)} all-gather(bf16[128,256]{1,0:T(8,128)(2,1)S(1)} %convert_element_type.266), channel_id=1, replica_groups=mesh['dp'=8,'mp'=4] {'dp'}, dimensions={0}, use_global_device_ids=true | all-gather | bytes 589824 | tf_op jit(solution)/shard_map/all_gather | solution.py:352
  102.8 30.8 %all-reduce.10.cloned.1.call-done = bf16[512,1024]{1,0:T(8,128)(2,1)} async-done(((bf16[512,1024]{1,0:T(8,128)(2,1)}), bf16[512,1024]{1,0:T(8,128)(2,1)}) %all-reduce.10.cloned.1.call-update) | async-done | bytes 1048592 | tf_op jit(solution)/shard_map/psum | solution.py:132
  136.2 50.0 %all-gather.7.cloned.1.call-done = bf16[1024,1024]{1,0:T(8,128)(2,1)} async-done(((bf16[128,1024]{1,0:T(8,128)(2,1)}), bf16[1024,1024]{1,0:T(8,128)(2,1)}) %all-gather.7.cloned.1.call-update) | async-done | bytes 2097168 | tf_op jit(solution)/shard_map/all_gather | solution.py:353
  186.2 4.3 fusion.79
  190.5 46.3 %all-gather.9.cloned.1.call-done = bf16[1024,1024]{1,0:T(8,128)(2,1)} async-done(((bf16[128,1024]{1,0:T(8,128)(2,1)}), bf16[1024,1024]{1,0:T(8,128)(2,1)}) %all-gather.9.cloned.1.call-update) | async-done | bytes 2097168 | tf_op jit(solution)/shard_map/all_gather | solution.py:354
  236.8 4.7 convolution_convert_fusion.6
  241.5 10.3 %all-reduce.14.cloned.1.call-start = ((), (), s32[]{:S(2)}) async-start(), calls=%async_computation.9 | async-start | bytes 2097152 | tf_op jit(solution)/shard_map/psum | solution.py:132
  251.8 24.5 %all-reduce.12.cloned.1.call-done = bf16[512,1024]{1,0:T(8,128)(2,1)} async-done(((bf16[512,1024]{1,0:T(8,128)(2,1)}), bf16[512,1024]{1,0:T(8,128)(2,1)}) %all-reduce.12.cloned.1.call-update) | async-done | bytes 1048592 | tf_op jit(solution)/shard_map/psum | solution.py:139
  288.6 4.5 fusion.107
  298.1 36.5 %all-reduce.14.cloned.1.call-done = bf16[512,1024]{1,0:T(8,128)(2,1)} async-done(((bf16[512,1024]{1,0:T(8,128)(2,1)}), bf16[512,1024]{1,0:T(8,128)(2,1)}) %all-reduce.14.cloned.1.call-update) | async-done | bytes 1048592 | tf_op jit(solution)/shard_map/psum | solution.py:132
  344.9 36.6 %all-reduce.16.cloned.1.call-done = bf16[512,1024]{1,0:T(8,128)(2,1)} async-done(((bf16[512,1024]{1,0:T(8,128)(2,1)}), bf16[512,1024]{1,0:T(8,128)(2,1)}) %all-reduce.16.cloned.1.call-update) | async-done | bytes 1048592 | tf_op jit(solution)/shard_map/psum | solution.py:139
  395.4 36.4 %all-reduce.18.cloned.1.call-done = bf16[512,1024]{1,0:T(8,128)(2,1)} async-done(((bf16[512,1024]{1,0:T(8,128)(2,1)}), bf16[512,1024]{1,0:T(8,128)(2,1)}) %all-reduce.18.cloned.1.call-update) | async-done | bytes 1048592 | tf_op jit(solution)/shard_map/psum | solution.py:189
  445.9 36.6 %all-reduce.20.cloned.1.call-done = bf16[512,1024]{1,0:T(8,128)(2,1)} async-done(((bf16[512,1024]{1,0:T(8,128)(2,1)}), bf16[512,1024]{1,0:T(8,128)(2,1)}) %all-reduce.20.cloned.1.call-update) | async-done | bytes 1048592 | tf_op jit(solution)/shard_map/psum | solution.py:223
  495.8 36.2 %all-reduce.22.cloned.1.call-done = bf16[512,1024]{1,0:T(8,128)(2,1)} async-done(((bf16[512,1024]{1,0:T(8,128)(2,1)}), bf16[512,1024]{1,0:T(8,128)(2,1)}) %all-reduce.22.cloned.1.call-update) | async-done | bytes 1048592 | tf_op jit(solution)/shard_map/psum | solution.py:189
  548.8 4.7 fusion.50
  558.2 5.3 convolution_add_fusion.2
  570.7 4.0 fusion.70
  586.1 43.5 %all-reduce = f32[32,384]{0,1:T(8,128)S(1)} all-reduce(f32[32,384]{0,1:T(8,128)S(1)} %reshape.589), channel_id=10, replica_groups=mesh['dp'=8,'mp'=4] {'dp','mp'}, use_global_device_ids=true, to_apply=%region_61.62.clone | all-reduce | flops 12288 | bytes 98304
  630.3 18.5 %reduce-scatter.8.cloned.1.call-done = f32[128,256]{1,0:T(8,128)} async-done(((f32[1024,256]{1,0:T(8,128)}), f32[128,256]{1,0:T(8,128)}) %reduce-scatter.8.cloned.1.call-update) | async-done | bytes 131088 | tf_op jit(solution)/shard_map/reduce_scatter | solution.py:375
  650.3 76.4 %reduce-scatter.6.cloned.1.call-done = f32[128,3,256]{2,0,1:T(8,128)} async-done(((f32[1024,3,256]{2,0,1:T(8,128)}), f32[128,3,256]{2,0,1:T(8,128)}) %reduce-scatter.6.cloned.1.call-update) | async-done | bytes 393232 | tf_op jit(solution)/shard_map/reduce_scatter | solution.py:374
  729.7 88.0 %reduce-scatter.10.cloned.1.call-done = f32[128,1024]{1,0:T(8,128)} async-done(((f32[1024,1024]{1,0:T(8,128)}), f32[128,1024]{1,0:T(8,128)}) %reduce-scatter.10.cloned.1.call-update) | async-done | bytes 524304 | tf_op jit(solution)/shard_map/reduce_scatter | solution.py:376
  820.1 88.9 %reduce-scatter.12.cloned.1.call-done = f32[128,1024]{1,0:T(8,128)} async-done(((f32[1024,1024]{1,0:T(8,128)}), f32[128,1024]{1,0:T(8,128)}) %reduce-scatter.12.cloned.1.call-update) | async-done | bytes 524304 | tf_op jit(solution)/shard_map/reduce_scatter | solution.py:377
  912.1 40.6 %psum.71 = f32[]{:T(128)} all-reduce(f32[]{:T(128)S(6)} %add.433), channel_id=1, replica_groups=mesh['dp'=8,'mp'=4] {'dp','mp'}, use_global_device_ids=true, to_apply=%region_63.64 | all-reduce | flops 1 | bytes 8 | tf_op jit(solution)/shard_map/psum | solution.py:398
  (378 shorter events, 149.6 us)
Async XLA Ops:
  7.2 377.3 %copy-start = (bf16[1,96,1024]{2,1,0:T(8,128)(2,1)S(1)}, bf16[1,96,1024]{2,1,0:T(8,128)(2,1)}, u32[]{:S(2)}) copy-start(bf16[1,96,1024]{2,1,0:T(8,128)(2,1)} %param.29) | copy-start | bytes 589828
  7.2 81.8 %all-gather.5.cloned.1.call-start = ((), (), s32[]{:S(2)}) async-start(), calls=%async_computation.4 | async-start | bytes 1769472 | tf_op jit(solution)/shard_map/all_gather | solution.py:351
  9.1 46.0 %copy-start.59 = (f32[128,256]{1,0:T(8,128)S(1)}, f32[128,256]{1,0:T(8,128)}, u32[]{:S(2)}) copy-start(f32[128,256]{1,0:T(8,128)} %param.34) | copy-start | bytes 393220
  9.1 124.4 %all-reduce.10.cloned.1.call-start = ((), (), s32[]{:S(2)}) async-start(), calls=%async_computation.5 | async-start | bytes 2097152 | tf_op jit(solution)/shard_map/psum | solution.py:132
  55.7 36.5 %copy-start.81 = (f32[256,1]{0,1:T(1,128)}, f32[256,1]{0,1:T(1,128)S(1)}, u32[]{:S(2)}) copy-start(f32[256,1]{0,1:T(1,128)S(1)} %get-tuple-element.294) | copy-start | bytes 3076
  101.1 85.1 %all-gather.7.cloned.1.call-start = ((), (), s32[]{:S(2)}) async-start(), calls=%async_computation.6 | async-start | bytes 2359296 | tf_op jit(solution)/shard_map/all_gather | solution.py:353
  101.9 134.9 %all-gather.9.cloned.1.call-start = ((), (), s32[]{:S(2)}) async-start(), calls=%async_computation.7 | async-start | bytes 2359296 | tf_op jit(solution)/shard_map/all_gather | solution.py:354
  102.7 173.5 %all-reduce.12.cloned.1.call-start = ((), (), s32[]{:S(2)}) async-start(), calls=%async_computation.8 | async-start | bytes 2097152 | tf_op jit(solution)/shard_map/psum | solution.py:139
  190.5 85.7 %copy-start.73 = (f32[1024,1]{0,1:T(1,128)S(1)}, f32[1024,1]{0,1:T(1,128)}, u32[]{:S(2)}) copy-start(f32[1024,1]{0,1:T(1,128)} %get-tuple-element.274) | copy-start | bytes 12292
  241.5 93.1 %all-reduce.14.cloned.1.call-start = ((), (), s32[]{:S(2)}) async-start(), calls=%async_computation.9 | async-start | bytes 2097152 | tf_op jit(solution)/shard_map/psum | solution.py:132
  295.9 38.8 %copy-start.74 = (f32[1024,1]{0,1:T(1,128)S(1)}, f32[1024,1]{0,1:T(1,128)}, u32[]{:S(2)}) copy-start(f32[1024,1]{0,1:T(1,128)} %get-tuple-element.277) | copy-start | bytes 12292
  298.1 83.4 %all-reduce.16.cloned.1.call-start = ((), (), s32[]{:S(2)}) async-start(), calls=%async_computation.10 | async-start | bytes 2097152 | tf_op jit(solution)/shard_map/psum | solution.py:139
  344.8 86.9 %all-reduce.18.cloned.1.call-start = ((), (), s32[]{:S(2)}) async-start(), calls=%async_computation.11 | async-start | bytes 2097152 | tf_op jit(solution)/shard_map/psum | solution.py:189
  395.1 87.4 %all-reduce.20.cloned.1.call-start = ((), (), s32[]{:S(2)}) async-start(), calls=%async_computation.12 | async-start | bytes 2097152 | tf_op jit(solution)/shard_map/psum | solution.py:223
  445.8 86.2 %all-reduce.22.cloned.1.call-start = ((), (), s32[]{:S(2)}) async-start(), calls=%async_computation.13 | async-start | bytes 2097152 | tf_op jit(solution)/shard_map/psum | solution.py:189
  495.3 86.5 %all-reduce.24.cloned.1.call-start = ((), (), s32[]{:S(2)}) async-start(), calls=%async_computation.14 | async-start | bytes 2097152 | tf_op jit(solution)/shard_map/psum | solution.py:223
  544.7 104.0 %reduce-scatter.8.cloned.1.call-start = ((), (), s32[]{:S(2)}) async-start(), calls=%async_computation.16 | async-start | bytes 1179648 | tf_op jit(solution)/shard_map/reduce_scatter | solution.py:375
  548.7 178.0 %reduce-scatter.6.cloned.1.call-start = ((), (), s32[]{:S(2)}) async-start(), calls=%async_computation.15 | async-start | bytes 3538944 | tf_op jit(solution)/shard_map/reduce_scatter | solution.py:374
  563.5 254.2 %reduce-scatter.10.cloned.1.call-start = ((), (), s32[]{:S(2)}) async-start(), calls=%async_computation.17 | async-start | bytes 4718592 | tf_op jit(solution)/shard_map/reduce_scatter | solution.py:376
  570.7 338.4 %reduce-scatter.12.cloned.1.call-start = ((), (), s32[]{:S(2)}) async-start(), calls=%async_computation.18 | async-start | bytes 4718592 | tf_op jit(solution)/shard_map/reduce_scatter | solution.py:377
  585.6 368.4 %copy-start.31 = (f32[128,3,256]{2,0,1:T(8,128)S(1)}, f32[128,3,256]{2,0,1:T(8,128)}, u32[]{:S(2)}) copy-start(f32[128,3,256]{2,0,1:T(8,128)} %param.30) | copy-start | bytes 1179652
  586.1 367.9 %copy-start.61 = (f32[128,3,256]{2,0,1:T(8,128)S(1)}, f32[128,3,256]{2,0,1:T(8,128)}, u32[]{:S(2)}) copy-start(f32[128,3,256]{2,0,1:T(8,128)} %param.31) | copy-start | bytes 1179652
  586.1 367.9 %copy-start.62 = (f32[128,3,256]{2,0,1:T(8,128)S(1)}, f32[128,3,256]{2,0,1:T(8,128)}, u32[]{:S(2)}) copy-start(f32[128,3,256]{2,0,1:T(8,128)} %param.32) | copy-start | bytes 1179652
  729.7 226.6 %copy-start.63 = (f32[128,3,256]{2,0,1:T(8,128)S(1)}, f32[128,3,256]{2,0,1:T(8,128)}, u32[]{:S(2)}) copy-start(f32[128,3,256]{2,0,1:T(8,128)} %param.33) | copy-start | bytes 1179652
  (93 other events, 366.7 us)
Sparse Core Ops, SparseCore 0:
  10.7 48.3 all-gather.4
  101.2 32.3 all-reduce.9
  136.5 49.6 all-gather.6
  189.0 47.7 all-gather.8
  241.6 34.5 all-reduce.11
  298.2 36.4 all-reduce.13
  345.0 36.4 all-reduce.15
  395.2 36.4 all-reduce.17
  445.9 36.4 all-reduce.19
  495.5 36.4 all-reduce.21
  544.9 36.4 all-reduce.23
  584.6 64.0 reduce-scatter.7
  652.8 73.8 reduce-scatter.5
  730.6 87.0 reduce-scatter.9
  821.2 87.8 reduce-scatter.11
where the time goes:
time: 981 us; the launch traced here: 973 us
  waiting for transfers between devices  606 us (62%)
  blocking collectives  159 us (16%)
  matrix products  85.3 us (9%)
  other arithmetic  57 us (6%)
  local copies, waits for them, and re-layouts  33.2 us (3%)
  between operations  20.6 us (2%)
  starting transfers between devices  11.7 us (1%)
    reduce_scatter x1, waiting for transfers between devices, per_device(): lax.psum_scatter(matrix_back[3], 'dp', scatter_dimension=0, tiled=True)  88.9 us
    reduce_scatter x1, waiting for transfers between devices, per_device(): lax.psum_scatter(matrix_back[2], 'dp', scatter_dimension=0, tiled=True)  88 us
    reduce_scatter x1, waiting for transfers between devices, per_device(): lax.psum_scatter(matrix_back[0], 'dp', scatter_dimension=0, tiled=True)  76.4 us
    psum x2, waiting for transfers between devices, backward_step(): lax.psum(over_columns(back_expanded, expand_full).astype(jnp.bfloat16), '...  72.6 us
    psum x2, waiting for transfers between devices, forward_step(): lax.psum(over_columns(context, rejoin_full).astype(jnp.bfloat16), 'mp')  67.3 us
    psum x2, waiting for transfers between devices, forward_step(): lax.psum(over_columns(active, narrow_full).astype(jnp.bfloat16), 'mp')  61.1 us
    all_gather x1, waiting for transfers between devices, per_device(): lax.all_gather(low_expand, 'dp', axis=0, tiled=True)  50 us
    all_gather x1, waiting for transfers between devices, per_device(): lax.all_gather(low_narrow, 'dp', axis=0, tiled=True)  46.3 us
  transfers between devices with their start and end apart: 15, of which 13 were waited for; matrix products, arithmetic and copies ran while one was open for 6% of the time, Pallas kernels for 0%

commit v1 on v0

v1 whole, which is shorter than its diff:
```python
import math
from types import SimpleNamespace

import jax
import jax.numpy as jnp
from jax import lax
from jax.experimental import pallas as pl
from jax.experimental.pallas import tpu as pltpu
from jax.sharding import PartitionSpec as P

HEAD_DIM = 64
SEQ_LEN = 512
DEPTH = 2
STEP = 7
EPS = 1e-05
BF = jnp.bfloat16
F32 = jnp.float32
MESH = pl.DeviceIdType.MESH
LANES = 128
TILE = 256
SLOTS = 128
CHUNKS = 2
SUB = 64
VEC, ATT, REJ, EXP, NAR = range(5)
GELU_A = 0.7978845608028654
GELU_B = 0.044715


def nn(former, latter):
    return jnp.dot(former, latter, preferred_element_type=F32)


def nt(former, latter):
    return lax.dot_general(former, latter, (((1,), (1,)), ((), ())), preferred_element_type=F32)


def low_transpose(block):
    return jnp.transpose(block.astype(F32), (1, 0)).astype(BF)


def loop(count, body):
    def step(index, carry):
        body(index)
        return carry

    lax.fori_loop(0, count, step, 0)


def each(first, last, body):
    if last - first <= 8:
        for index in range(first, last):
            body(index)
    else:

        def step(index, carry):
            body(index)
            return carry

        lax.fori_loop(first, last, step, 0)


def aligned(index, size):
    return pl.ds(pl.multiple_of(index, size), size)


def layer_kernel(names, sizes, *refs):
    r = SimpleNamespace(**dict(zip(names, refs, strict=True)))
    n, d_model, rows, hw, uw, vr = sizes
    half = rows // 2
    ch = half // CHUNKS
    lines = n // 2
    heads = hw // HEAD_DIM
    slot_half = SLOTS // 2

    d = lax.axis_index("dp")
    m = lax.axis_index("mp")
    z, y = d // 2, d % 2
    core = m % 2
    core_peer = (d, m + 1 - 2 * core)
    x_peer = (d, (m + 2) % 4)
    y_peer = (d + 1 - 2 * y, m)
    own0 = core * half
    oth0 = half - own0

    weights = (r.wv, r.wa, r.wr, r.we, r.wn)
    grads = (r.gsv, r.gsa, r.gsr, r.gse, r.gsn)
    from_y = (r.yv, r.ya, r.yr, r.ye, r.yn)
    from_z = (r.zv, r.za, r.zr, r.ze, r.zn)

    def z_peer(step):
        return (((z + step) % lines) * 2 + y, m)

    def z_from(step):
        return ((z + lines - step) % lines) * 2 + y

    def block(ref, region, index):
        where = aligned(index * vr, vr)
        return ref.at[:, where, :] if region == ATT else ref.at[where, :]

    def remote(source, target, send, recv, device):
        return pltpu.make_async_remote_copy(
            src_ref=source,
            dst_ref=target,
            send_sem=send,
            recv_sem=recv,
            device_id=device,
            device_id_type=MESH,
        )

    barrier = pltpu.get_barrier_semaphore()
    for peer in (core_peer, x_peer, y_peer):
        pl.semaphore_signal(barrier, inc=1, device_id=peer, device_id_type=MESH)
    each(
        1,
        lines,
        lambda s: pl.semaphore_signal(barrier, inc=1, device_id=z_peer(s), device_id_type=MESH),
    )
    pl.semaphore_wait(barrier, 3 + lines - 1)

    def gather_z(region, step):
        piece = block(weights[region], region, d)
        return remote(
            piece, piece, r.agzs.at[region, step], r.agzr.at[region, step], z_peer(step)
        )

    def gather_z_arrival(region, step):
        piece = block(weights[region], region, z_from(step))
        return remote(
            piece, piece, r.agzs.at[region, step], r.agzr.at[region, step], z_peer(step)
        )

    def gather_y(region, step):
        piece = block(weights[region], region, z_from(step))
        return remote(piece, piece, r.agys.at[region, step], r.agyr.at[region, step], y_peer)

    def gather_y_arrival(region, step):
        piece = block(weights[region], region, z_from(step) + 1 - 2 * y)
        return remote(piece, piece, r.agys.at[region, step], r.agyr.at[region, step], y_peer)

    def gather_start(region):
        each(1, lines, lambda s: gather_z(region, s).start())
        gather_y(region, 0).start()

    def gather_pass(region):
        def one(step):
            gather_z_arrival(region, step).wait_recv()
            gather_y(region, step).start()

        each(1, lines, one)

    def gather_wait(region):
        each(0, lines, lambda s: gather_y_arrival(region, s).wait_recv())

    def gather_close(region):
        each(1, lines, lambda s: gather_z(region, s).wait_send())
        each(0, lines, lambda s: gather_y(region, s).wait_send())

    def scatter_y(region, step):
        owner = ((z + step) % lines) * 2 + 1 - y
        return remote(
            block(grads[region], region, owner),
            from_y[region].at[step],
            r.rsys.at[region, step],
            r.rsyr.at[region, step],
            y_peer,
        )

    def scatter_z(region, step):
        owner = ((z + step) % lines) * 2 + y
        return remote(
            block(grads[region], region, owner),
            from_z[region].at[step - 1],
            r.rszs.at[region, step],
            r.rszr.at[region, step],
            z_peer(step),
        )

    def scatter_start(region):
        def one(step):
            scatter_y(region, step).start()

        each(1, lines, one)
        one(0)

    def scatter_pass(region, step):
        scatter_y(region, step).wait_recv()
        piece = block(grads[region], region, ((z + step) % lines) * 2 + y)
        piece[...] = (piece[...].astype(F32) + from_y[region][step].astype(F32)).astype(BF)
        scatter_z(region, step).start()

    def scatter_finish(region, out_ref):
        scatter_y(region, 0).wait_recv()
        piece = block(grads[region], region, d)
        out_ref[...] = piece[...].astype(F32) + from_y[region][0].astype(F32)

        def one(step):
            scatter_z(region, step).wait_recv()
            out_ref[...] += from_z[region][step - 1].astype(F32)

        each(1, lines, one)

    def scatter_close(region):
        each(0, lines, lambda s: scatter_y(region, s).wait_send())
        each(1, lines, lambda s: scatter_z(region, s).wait_send())

    def core_copy(k, q, count):
        b = k % 2
        return remote(
            r.cs.at[b, q, :count],
            r.cr.at[b, q, :count],
            r.arcs.at[k, q],
            r.arcr.at[k, q],
            core_peer,
        )

    def x_copy(k, q, count):
        b = k % 2
        return remote(
            r.xs.at[b, q, :count],
            r.xr.at[b, q, :count],
            r.arxs.at[k, q],
            r.arxr.at[k, q],
            x_peer,
        )

    def sum_begin(k, q, tile_of, count):
        b = k % 2

        def one(j):
            cols = aligned(j * TILE, TILE)
            part = tile_of(cols)
            r.cs[b, q, :count, cols] = part[:count].astype(BF)
            r.acc[:count, cols] = part[count:]

        loop(d_model // TILE, one)
        copy = core_copy(k, q, count)
        copy.start()
        copy.wait_recv()
        r.xs[b, q, :count] = (r.acc[:count] + r.cr[b, q, :count].astype(F32)).astype(BF)
        x_copy(k, q, count).start()

    def sum_end(k, q, count):
        x_copy(k, q, count).wait()
        core_copy(k, q, count).wait_send()

    def sum_rows(k, q, where):
        b = k % 2
        return r.xs[b, q, where].astype(F32) + r.xr[b, q, where].astype(F32)

    def share(k, ref, q):
        where = aligned(own0 + q * ch, ch)
        return remote(ref.at[where], ref.at[where], r.shs.at[k, q], r.shr.at[k, q], core_peer)

    def share_arrival(k, ref, q):
        where = aligned(oth0 + q * ch, ch)
        return remote(ref.at[where], ref.at[where], r.shs.at[k, q], r.shr.at[k, q], core_peer)

    def share_wait(k, ref, q):
        share(k, ref, q).wait_send()
        share_arrival(k, ref, q).wait_recv()

    def both(ref, q, cols=slice(None)):
        return jnp.concatenate(
            [ref[aligned(oth0 + q * ch, ch), cols], ref[aligned(own0 + q * ch, ch), cols]],
            axis=0,
        )

    def put_both(ref, q, cols, value):
        ref[aligned(oth0 + q * ch, ch), cols] = value[:ch]
        ref[aligned(own0 + q * ch, ch), cols] = value[ch:]

    r.vb[0] = r.vin[...].astype(BF)
    swap = remote(r.vb.at[0], r.vb.at[1], r.vxs.at[0], r.vxr.at[0], core_peer)
    swap.start()
    mine = aligned(d * vr, vr)
    r.wa[:, mine, :] = r.attend[...].astype(BF)
    gather_start(ATT)
    r.wr[mine, :] = r.rejoin[...].astype(BF)
    swap.wait_recv()
    r.vb[2] = r.vb[0] + r.vb[1]
    swap_x = remote(r.vb.at[2], r.vb.at[3], r.vxs.at[1], r.vxr.at[1], x_peer)
    swap_x.start()
    r.we[mine, :] = r.expand[...].astype(BF)
    r.wn[mine, :] = r.narrow[...].astype(BF)
    swap_x.wait_recv()
    r.wv[mine, :] = r.vb[2] + r.vb[3]
    gather_start(VEC)
    gather_start(REJ)

    r.pb[...] = jnp.full(r.pb.shape, SEQ_LEN, jnp.int32)
    slots = r.pos.shape[1]
    r.pb[0:1, 0:slots] = r.pos[...]
    r.pb[8:9, 0:slots] = r.cho[...]
    pos_row = jnp.broadcast_to(r.pb[0:1, :], (SLOTS, SLOTS))
    cho_row = jnp.broadcast_to(r.pb[8:9, :], (SLOTS, SLOTS))
    pos_col = jnp.transpose(pos_row.astype(F32), (1, 0)).astype(jnp.int32)
    cho_col = jnp.transpose(cho_row.astype(F32), (1, 0)).astype(jnp.int32)
    lane_iota = lax.broadcasted_iota(jnp.int32, (SLOTS, LANES), 1)
    row_iota = lax.broadcasted_iota(jnp.int32, (SLOTS, LANES), 0)
    for j in range(rows // LANES):
        r.oh[:, j * LANES : (j + 1) * LANES] = jnp.where(
            pos_col == lane_iota + j * LANES, 1.0, 0.0
        ).astype(BF)
        r.oht[j * LANES : (j + 1) * LANES, :] = jnp.where(
            pos_row == row_iota + j * LANES, 1.0, 0.0
        ).astype(BF)
    r.low2c[...] = jnp.zeros(r.low2c.shape, BF)
    r.low2c[0 : r.table.shape[0], :] = r.table[...]
    choice = jnp.where(cho_col == lane_iota, 1.0, 0.0).astype(BF)
    for j in range(d_model // TILE):
        r.slt[:, j * TILE : (j + 1) * TILE] = nn(
            choice, r.low2c[:, j * TILE : (j + 1) * TILE]
        ).astype(BF)
    r.mc[...] = jnp.zeros(r.mc.shape, BF)
    r.mc[0:slots, :] = r.mcot[...].reshape(slots, d_model)
    r.vg[...] = jnp.zeros(r.vg.shape, F32)

    def embed(i):
        where = aligned(i * SUB, SUB)
        hot = r.oht[where, :]
        keep = 1.0 - jnp.sum(hot.astype(F32), axis=1, keepdims=True)
        r.keep[where, :] = keep
        r.xl[where, :] = (r.tok[where, :].astype(F32) * keep + nn(hot, r.slt[...])).astype(BF)

    loop(rows // SUB, embed)
    r.st[...] = r.xl[aligned(own0, half), :].astype(F32)

    def transpose_into(target, lane0, source, row0, count):
        for i in range(count // LANES):
            target[:, lane0 + i * LANES : lane0 + (i + 1) * LANES] = low_transpose(
                source[row0 + i * LANES : row0 + (i + 1) * LANES, :]
            )

    transpose_into(r.xt, 0, r.xl, 0, rows)

    gather_pass(ATT)
    gather_start(EXP)
    gather_pass(VEC)
    gather_wait(ATT)
    gather_wait(VEC)
    for j in range(d_model // LANES):
        r.vt[:, j * LANES : (j + 1) * LANES] = jnp.transpose(
            r.wv[j * LANES : (j + 1) * LANES, :].astype(F32), (1, 0)
        )[0:16, :]

    def head_bias(row):
        return r.vt[row : row + 1, aligned(m * hw, hw)]

    half_mask = lax.broadcasted_iota(jnp.int32, (1, LANES), 1) < HEAD_DIM

    def lane_half(value, head):
        return jnp.where(half_mask if head % 2 == 0 else jnp.logical_not(half_mask), value, 0)

    def put_heads(ref, q, value):
        for head in range(heads):
            pair = (head // 2) * LANES
            piece = lane_half(value[:, pair : pair + LANES], head)
            ref[head, aligned(oth0 + q * ch, ch), :] = piece[:ch]
            ref[head, aligned(own0 + q * ch, ch), :] = piece[ch:]

    def put_heads_across(ref, q, across):
        for head in range(heads):
            at = (head % 2) * HEAD_DIM
            piece = across[head * HEAD_DIM : (head + 1) * HEAD_DIM, :]
            ref[head, at : at + HEAD_DIM, aligned(oth0 + q * ch, ch)] = piece[:, :ch]
            ref[head, at : at + HEAD_DIM, aligned(own0 + q * ch, ch)] = piece[:, ch:]

    def put_across(ref, q, across):
        ref[:, aligned(oth0 + q * ch, ch)] = across[:, :ch]
        ref[:, aligned(own0 + q * ch, ch)] = across[:, ch:]

    for ref in (r.qzt, r.dozt):
        ref[...] = jnp.zeros(ref.shape, BF)

    def share_block(layer, head, lane0):
        if layer == 0:
            return r.p0.at[head, :, aligned(lane0, TILE)]
        return r.gse.at[
            aligned((head // 2) * rows, rows), aligned((head % 2) * rows + lane0, TILE)
        ]

    def project(layer, q):
        x = both(r.xl, q)
        queries = (nn(x, r.wa[0]) + head_bias(0)).astype(BF) * jnp.asarray(0.125, BF)
        put_heads(r.qz.at[layer], q, queries)
        put_heads_across(r.qzt.at[layer], q, low_transpose(queries))
        keys = nn(x, r.wa[1]).astype(BF)
        put_both(r.kn.at[layer], q, slice(None), keys)
        put_across(r.kt.at[layer], q, low_transpose(keys))
        values = (nn(x, r.wa[2]) + head_bias(1)).astype(BF)
        put_both(r.vn.at[layer], q, slice(None), values)
        put_across(r.vvt, q, low_transpose(values))

    def attend_forward(layer):
        def one(i):
            head, lane0 = i // 2, (i % 2) * TILE
            pair = aligned((head // 2) * LANES, LANES)
            lanes = aligned(lane0, TILE)
            scores = nn(r.kn[layer, :, pair], r.qzt[layer, head, :, lanes])
            raised = jnp.exp(scores - jnp.max(scores, axis=0, keepdims=True))
            total = jnp.sum(raised, axis=0, keepdims=True)
            low = (raised * (1.0 / total)).astype(BF)
            share_block(layer, head, lane0)[...] = low
            where = aligned(head * HEAD_DIM, HEAD_DIM)
            r.ct[layer, where, lanes] = nn(r.vvt[where, :], low).astype(BF)

        loop(heads * (rows // TILE), one)
        target, row0 = (r.ctx, 0) if layer == 0 else (r.ctx1, 0)
        for i in range(rows // LANES):
            target[row0 + i * LANES : row0 + (i + 1) * LANES, :] = low_transpose(
                r.ct[layer, :, i * LANES : (i + 1) * LANES]
            )

    def first_norm(layer, q):
        def one(i):
            at = aligned(q * ch + i * SUB, SUB)
            total = sum_rows(2 * layer, q, aligned(i * SUB, SUB))
            res = r.st[at, :] + (total + r.vt[2:3, :])
            cen = res - jnp.mean(res, axis=1, keepdims=True)
            spread = lax.rsqrt(jnp.mean(cen * cen, axis=1, keepdims=True) + EPS)
            hat = cen * spread
            r.xh1[layer, at, :] = hat
            r.rs1[layer, at, :] = spread
            normed = hat * r.vt[4:5, :] + r.vt[5:6, :]
            r.st[at, :] = normed
            r.normed[aligned(own0 + q * ch + i * SUB, SUB), :] = normed.astype(BF)

        loop(ch // SUB, one)

    def second_norm(layer, q):
        def one(i):
            at = aligned(q * ch + i * SUB, SUB)
            total = sum_rows(2 * layer + 1, q, aligned(i * SUB, SUB))
            res = r.st[at, :] + (total + r.vt[3:4, :])
            cen = res - jnp.mean(res, axis=1, keepdims=True)
            spread = lax.rsqrt(jnp.mean(cen * cen, axis=1, keepdims=True) + EPS)
            hat = cen * spread
            r.xh2[layer, at, :] = hat
            r.rs2[layer, at, :] = spread
            out = hat * r.vt[6:7, :] + r.vt[7:8, :]
            r.st[at, :] = out
            if layer < DEPTH - 1:
                r.xl[aligned(own0 + q * ch + i * SUB, SUB), :] = out.astype(BF)

        loop(ch // SUB, one)

    def unit_act(layer):
        return r.act0 if layer == 0 else r.gsn

    def unit_slope(layer):
        return (r.slope0, 0) if layer == 0 else (r.gsn, rows)

    def widen(layer, q):
        act = unit_act(layer)
        slope, slope0 = unit_slope(layer)

        def one(j):
            cols = aligned(j * TILE, TILE)
            v = nn(both(r.normed, q), r.we[:, cols]) + r.vt[pl.ds(8 + m, 1), cols]
            square = v * v
            t = jnp.tanh(GELU_A * v * (1.0 + GELU_B * square))
            gate = 0.5 * (1.0 + t)
            put_both(act, q, cols, (v * gate).astype(BF))
            bend = gate + (0.5 * GELU_A) * v * (1.0 - t * t) * (1.0 + (3.0 * GELU_B) * square)
            bend = bend.astype(BF)
            slope[aligned(slope0 + oth0 + q * ch, ch), cols] = bend[:ch]
            slope[aligned(slope0 + own0 + q * ch, ch), cols] = bend[ch:]

        loop(uw // TILE, one)

    def rejoin_sum(layer, q):
        ctx = r.ctx if layer == 0 else r.ctx1
        sum_begin(2 * layer, q, lambda cols: nt(both(ctx, q), r.wr[cols, :]), ch)

    def narrow_sum(layer, q):
        act = unit_act(layer)
        sum_begin(2 * layer + 1, q, lambda cols: nt(both(act, q), r.wn[cols, :]), ch)

    for layer in range(DEPTH):
        for q in range(CHUNKS):
            if layer > 0:
                share_wait(2 * layer - 1, r.xl, q)
            project(layer, q)
        if layer == 0:
            gather_pass(REJ)
        attend_forward(layer)
        if layer == 0:
            gather_wait(REJ)
        for q in range(CHUNKS):
            rejoin_sum(layer, q)
        if layer == 0:
            gather_start(NAR)
            gather_pass(EXP)
        else:
            transpose_into(r.xt, rows, r.xl, 0, rows)
        for q in range(CHUNKS):
            sum_end(2 * layer, q, ch)
            first_norm(layer, q)
            share(2 * layer, r.normed, q).start()
            if layer == 0 and q == 0:
                gather_wait(EXP)
            share_wait(2 * layer, r.normed, q)
            widen(layer, q)
            if layer == 0 and q == 0:
                gather_pass(NAR)
                gather_wait(NAR)
            narrow_sum(layer, q)
        if layer == 0:
            transpose_into(r.nt, 0, r.normed, 0, rows)
        for q in range(CHUNKS):
            sum_end(2 * layer + 1, q, ch)
            second_norm(layer, q)
            if layer < DEPTH - 1:
                share(2 * layer + 1, r.xl, q).start()

    own_rows = aligned(own0, half)
    out_here = pltpu.make_async_copy(r.st, r.act.at[own_rows], r.osem.at[0])
    out_there = remote(r.st, r.act.at[own_rows], r.osem.at[1], r.osem.at[2], core_peer)
    out_arrival = remote(
        r.st, r.act.at[aligned(oth0, half)], r.osem.at[1], r.osem.at[2], core_peer
    )
    out_here.start()
    out_there.start()

    def add_rows(row, value):
        r.vg[row : row + 1, :] += jnp.sum(value, axis=0, keepdims=True)

    def norm_pull(g, hat, spread, gain):
        scaled = g * gain
        mean = jnp.mean(scaled, axis=1, keepdims=True)
        inner = jnp.mean(scaled * hat, axis=1, keepdims=True)
        return spread * (scaled - mean - hat * inner)

    def second_pull(layer, q, gradient):
        def one(i):
            at = aligned(q * ch + i * SUB, SUB)
            g = gradient(i, at)
            hat = r.xh2[layer, at, :]
            add_rows(6, g * hat)
            add_rows(7, g)
            back = norm_pull(g, hat, r.rs2[layer, at, :], r.vt[6:7, :])
            add_rows(3, back)
            r.gb[at, :] = back
            r.low2[aligned(own0 + q * ch + i * SUB, SUB), :] = back.astype(BF)

        loop(ch // SUB, one)

    def first_pull(layer, q, gradient):
        def one(i):
            at = aligned(q * ch + i * SUB, SUB)
            g = gradient(i, at)
            hat = r.xh1[layer, at, :]
            add_rows(4, g * hat)
            add_rows(5, g)
            back = norm_pull(g, hat, r.rs1[layer, at, :], r.vt[4:5, :])
            add_rows(2, back)
            r.gb[at, :] = back
            r.xl[aligned(own0 + q * ch + i * SUB, SUB), :] = back.astype(BF)

        loop(ch // SUB, one)

    def hot_rows(at_start):
        return r.oht[aligned(own0 + at_start, SUB), :]

    def bias_sums(row0):
        for kind, row in ((0, 0), (2, 1)):
            cols = aligned(m * hw, hw)
            r.vg[row : row + 1, cols] += jnp.sum(
                r.dp[kind, row0 : row0 + rows, :].astype(F32), axis=0, keepdims=True
            )

    for q in range(CHUNKS):
        second_pull(1, q, lambda i, at: nn(hot_rows(q * ch + i * SUB), r.mc[...]))
        share(4, r.low2, q).start()
    hot = r.oh[...]

    def pick(target, row0, source, source0, width):
        def one(j):
            cols = aligned(j * TILE, TILE)
            target[row0 : row0 + SLOTS, cols] = nn(
                hot, source[source0 : source0 + rows, cols]
            ).astype(BF)

        loop(width // TILE, one)

    pick(r.act0, rows, r.gsn, 0, uw)
    pick(r.slc, 0, r.gsn, rows, uw)
    pick(r.low2c, 0, r.normed, 0, d_model)
    transpose_into(r.nt, rows, r.low2c, 0, SLOTS)
    pick(r.ctx, rows, r.ctx1, 0, hw)
    for q in range(CHUNKS):
        share_wait(4, r.low2, q)
    pick(r.low2c, 0, r.low2, 0, d_model)

    def slot_units(j):
        cols = aligned(j * TILE, TILE)
        back = nn(r.low2c[...], r.wn[:, cols]) * r.slc[:, cols].astype(F32)
        back = back.astype(BF)
        r.be[rows : rows + SLOTS, cols] = back
        r.vg[pl.ds(8 + m, 1), cols] += jnp.sum(back.astype(F32), axis=0, keepdims=True)

    loop(uw // TILE, slot_units)
    slot_own = core * slot_half
    slot_oth = slot_half - slot_own

    def slot_tile(cols):
        part = nt(r.be[rows : rows + SLOTS, :], r.we[cols, :])
        r.part[...] = part
        return jnp.concatenate(
            [
                r.part[aligned(slot_oth, slot_half), :],
                r.part[aligned(slot_own, slot_half), :],
            ],
            axis=0,
        )

    sum_begin(4, 0, slot_tile, slot_half)
    transpose_into(r.l2t, rows, r.low2c, 0, SLOTS)
    sum_end(4, 0, slot_half)
    mine_slots = r.slt.at[aligned(slot_own, slot_half)]
    mine_slots[...] = sum_rows(4, 0, slice(0, slot_half)).astype(BF)
    slots_out = remote(mine_slots, mine_slots, r.osem.at[3], r.osem.at[4], core_peer)
    slots_in_ref = r.slt.at[aligned(slot_oth, slot_half)]
    slots_in = remote(slots_in_ref, slots_in_ref, r.osem.at[3], r.osem.at[4], core_peer)
    slots_out.start()
    slots_in.wait_recv()
    for q in range(CHUNKS):
        first_pull(
            1, q, lambda i, at: r.gb[at, :] + nn(hot_rows(q * ch + i * SUB), r.slt[...])
        )
        share(5, r.xl, q).start()

    for head in range(heads):
        r.qc[head] = nn(hot, r.qz[1, head]).astype(BF)
        source = r.gse[
            (head // 2) * rows : (head // 2 + 1) * rows,
            (head % 2) * rows : (head % 2 + 1) * rows,
        ]
        r.pc[head] = nn(source, r.oht[...]).astype(BF)
    r.cct[...] = nn(r.ct[1], r.oht[...]).astype(BF)
    for q in range(CHUNKS):
        share_wait(5, r.xl, q)
    pick(r.low2c, 0, r.xl, 0, d_model)
    transpose_into(r.l1t, rows, r.low2c, 0, SLOTS)
    low_ctx = nn(r.low2c[...], r.wr[...]).astype(BF)
    across = low_transpose(low_ctx)
    dq_across = []
    for pair in range(heads // 2):
        lanes = slice(pair * LANES, (pair + 1) * LANES)
        dv = jnp.zeros((rows, LANES), F32)
        dk = jnp.zeros((rows, LANES), F32)
        for head in (2 * pair, 2 * pair + 1):
            where = slice(head * HEAD_DIM, (head + 1) * HEAD_DIM)
            at = (head % 2) * HEAD_DIM
            r.dozt[head, at : at + HEAD_DIM, 0:SLOTS] = across[where, :]
            low = r.pc[head]
            dv += nn(low, lane_half(low_ctx[:, lanes], head))
            dp = nn(r.vn[1, :, lanes], r.dozt[head, :, 0:SLOTS])
            delta = jnp.sum(
                across[where, :].astype(F32) * r.cct[where, :].astype(F32), axis=0, keepdims=True
            )
            ds = (low.astype(F32) * (dp - delta)).astype(BF)
            dk += nn(ds, r.qc[head])
            dq_across.append(nn(r.kt[1, where, :], ds) * 0.125)
        r.dp[1, rows : 2 * rows, lanes] = dk.astype(BF)
        r.dp[2, rows : 2 * rows, lanes] = dv.astype(BF)
    dq = low_transpose(jnp.concatenate(dq_across, axis=0))
    r.dp[0, rows : 2 * rows, :] = nn(r.oht[...], dq).astype(BF)
    bias_sums(rows)

    def layer_rows(k, q, row0):
        def tile_of(cols):
            total = None
            for kind in range(3):
                lhs = jnp.concatenate(
                    [
                        r.dp[kind, aligned(row0 + oth0 + q * ch, ch), :],
                        r.dp[kind, aligned(row0 + own0 + q * ch, ch), :],
                    ],
                    axis=0,
                )
                part = nt(lhs, r.wa[kind, cols, :])
                total = part if total is None else total + part
            return total

        sum_begin(k, q, tile_of, ch)

    for q in range(CHUNKS):
        layer_rows(5, q, rows)

    for q in range(CHUNKS):
        sum_end(5, q, ch)
        second_pull(
            0, q, lambda i, at: r.gb[at, :] + sum_rows(5, q, aligned(i * SUB, SUB))
        )
        share(6, r.low2, q).start()
        share_wait(6, r.low2, q)

        def units(j, q=q):
            cols = aligned(j * TILE, TILE)
            slope = both(r.slope0, q, cols).astype(F32)
            back = (nn(both(r.low2, q), r.wn[:, cols]) * slope).astype(BF)
            put_both(r.be, q, cols, back)
            r.vg[pl.ds(8 + m, 1), cols] += jnp.sum(back.astype(F32), axis=0, keepdims=True)

        loop(uw // TILE, units)
        sum_begin(6, q, lambda cols, q=q: nt(both(r.be, q), r.we[cols, :]), ch)

    def weight_grad(target, across, latter, width):
        def one(t):
            i, j = t // (width // TILE), t % (width // TILE)
            at, cols = aligned(i * TILE, TILE), aligned(j * TILE, TILE)
            target[at, cols] = nn(across[at, :], latter[:, cols]).astype(BF)

        loop((d_model // TILE) * (width // TILE), one)

    transpose_into(r.l2t, 0, r.low2, 0, rows)
    weight_grad(r.gsn, r.l2t, r.act0, uw)
    scatter_start(NAR)
    weight_grad(r.gse, r.nt, r.be, uw)
    scatter_start(EXP)
    for q in range(CHUNKS):
        sum_end(6, q, ch)
        first_pull(
            0, q, lambda i, at: r.gb[at, :] + sum_rows(6, q, aligned(i * SUB, SUB))
        )
        share(7, r.xl, q).start()
    scatter_pass(NAR, 1) if lines > 1 else None
    for q in range(CHUNKS):
        share_wait(7, r.xl, q)
        back = nn(both(r.xl, q), r.wr[...]).astype(BF)
        put_heads(r.doz, q, back)
        put_heads_across(r.dozt, q, low_transpose(back))

    def head_pair(pair):
        lanes = aligned(pair * LANES, LANES)
        dv = jnp.zeros((rows, LANES), F32)
        dk = jnp.zeros((rows, LANES), F32)
        for side in range(2):
            head = 2 * pair + side
            where = aligned(head * HEAD_DIM, HEAD_DIM)
            for part in range(rows // TILE):
                some = slice(part * TILE, (part + 1) * TILE)
                low = r.p0[head, :, some]
                dv += nn(low, r.doz[head, some, :])
                inner = r.dozt[head, side * HEAD_DIM : (side + 1) * HEAD_DIM, some]
                delta = jnp.sum(
                    inner.astype(F32) * r.ct[0, where, some].astype(F32), axis=0, keepdims=True
                )
                dp = nn(r.vn[0, :, lanes], r.dozt[head, :, some])
                ds = (low.astype(F32) * (dp - delta)).astype(BF)
                dk += nn(ds, r.qz[0, head, some, :])
                r.dqt[where, some] = (nn(r.kt[0, where, :], ds) * 0.125).astype(BF)
        r.dp[1, 0:rows, lanes] = dk.astype(BF)
        r.dp[2, 0:rows, lanes] = dv.astype(BF)

    loop(heads // 2, head_pair)
    for i in range(rows // LANES):
        some = slice(i * LANES, (i + 1) * LANES)
        r.dp[0, some, :] = low_transpose(r.dqt[:, some])
    for q in range(CHUNKS):
        layer_rows(7, q, 0)
    bias_sums(0)
    transpose_into(r.l1t, 0, r.xl, 0, rows)
    weight_grad(r.gsr, r.l1t, r.ctx, hw)
    scatter_start(REJ)
    first_of_x = jnp.where(m < 2, 1.0, 0.0)
    r.vg[2:8, :] = r.vg[2:8, :] * first_of_x
    for j in range(d_model // LANES):
        tall = jnp.concatenate(
            [r.vg[:, j * LANES : (j + 1) * LANES], jnp.zeros((LANES - 16, LANES), F32)], axis=0
        )
        r.gsv[j * LANES : (j + 1) * LANES, :] = jnp.transpose(tall, (1, 0)).astype(BF)
    scatter_start(VEC)
    for kind in range(3):
        weight_grad(r.gsa.at[kind], r.xt, r.dp.at[kind], hw)
    scatter_start(ATT)
    each(2, lines, lambda s: scatter_pass(NAR, s))
    out_here.wait()
    out_there.wait_send()
    for q in range(CHUNKS):
        sum_end(7, q, ch)

        def last(i, q=q):
            at = aligned(q * ch + i * SUB, SUB)
            g = r.gb[at, :] + sum_rows(7, q, aligned(i * SUB, SUB))
            r.st[at, :] = g * r.keep[aligned(own0 + q * ch + i * SUB, SUB), :]

        loop(ch // SUB, last)
    in_here = pltpu.make_async_copy(r.st, r.ing.at[own_rows], r.osem.at[5])
    in_there = remote(r.st, r.ing.at[own_rows], r.osem.at[6], r.osem.at[7], core_peer)
    in_arrival = remote(r.st, r.ing.at[aligned(oth0, half)], r.osem.at[6], r.osem.at[7], core_peer)
    in_here.start()
    in_there.start()

    each(1, lines, lambda s: scatter_pass(EXP, s))
    each(1, lines, lambda s: scatter_pass(REJ, s))
    each(1, lines, lambda s: scatter_pass(VEC, s))
    each(1, lines, lambda s: scatter_pass(ATT, s))

    def squares(value):
        value = value * value
        if value.ndim == 3:
            value = jnp.sum(value, axis=0)
        value = jnp.sum(value, axis=0, keepdims=True)
        return jnp.sum(value, axis=1, keepdims=True)

    scatter_finish(NAR, r.gn)
    scatter_finish(EXP, r.ge)
    scatter_finish(REJ, r.gr)
    total = squares(r.gn[...]) + squares(r.ge[...]) + squares(r.gr[...])
    scatter_finish(VEC, r.vf.at[0])
    swap_v = remote(r.vf.at[0], r.vf.at[1], r.vxs.at[2], r.vxr.at[2], core_peer)
    swap_v.start()
    swap_v.wait_recv()
    r.vf[2] = r.vf[0] + r.vf[1]
    swap_w = remote(r.vf.at[2], r.vf.at[3], r.vxs.at[3], r.vxr.at[3], x_peer)
    swap_w.start()
    swap_w.wait_recv()
    r.gv[...] = r.vf[2] + r.vf[3]
    lane = lax.broadcasted_iota(jnp.int32, r.gv.shape, 1)
    own_lanes = jnp.logical_and(lane >= 3 * m, lane < 3 * m + 3)
    total = total + squares(jnp.where(own_lanes, r.gv[...], 0.0))
    scatter_finish(ATT, r.ga)
    total = total + squares(r.ga[...])

    r.ns[0] = jnp.broadcast_to(total, (8, LANES))
    for step, peer in enumerate((core_peer, x_peer, y_peer)):
        swap_n = remote(r.ns.at[step], r.nr.at[step], r.nss.at[step], r.nsr.at[step], peer)
        swap_n.start()
        swap_n.wait_recv()
        r.ns[step + 1] = r.ns[step] + r.nr[step]
    r.nz[z] = r.ns[3]

    def norm_copy(step):
        return remote(
            r.ns.at[3], r.nz.at[z], r.nzs.at[step], r.nzr.at[step], z_peer(step)
        )

    def norm_arrival(step):
        return remote(
            r.ns.at[3],
            r.nz.at[(z + lines - step) % lines],
            r.nzs.at[step],
            r.nzr.at[step],
            z_peer(step),
        )

    each(1, lines, lambda s: norm_copy(s).start())
    each(1, lines, lambda s: norm_arrival(s).wait_recv())
    r.norm[...] = jnp.sqrt(jnp.sum(r.nz[...], axis=0))

    each(1, lines, lambda s: norm_copy(s).wait_send())
    for step, peer in enumerate((core_peer, x_peer, y_peer)):
        remote(
            r.ns.at[step], r.nr.at[step], r.nss.at[step], r.nsr.at[step], peer
        ).wait_send()
    swap.wait_send()
    swap_x.wait_send()
    swap_v.wait_send()
    swap_w.wait_send()
    slots_out.wait_send()
    for region in range(5):
        gather_close(region)
        scatter_close(region)
    out_arrival.wait_recv()
    in_here.wait()
    in_there.wait_send()
    in_arrival.wait_recv()


def run_layers(
    n, tok, pos, cho, table, mcot, attend, rejoin, expand, narrow, vin
):
    rows, d_model = tok.shape
    vr = rejoin.shape[0]
    hw = rejoin.shape[1]
    uw = expand.shape[1]
    lines = n // 2
    ways = max(lines - 1, 1)
    half = rows // 2
    ch = half // CHUNKS
    heads = hw // HEAD_DIM
    wide = rows + SLOTS
    inputs = [
        ("tok", tok),
        ("pos", pos),
        ("cho", cho),
        ("table", table),
        ("mcot", mcot),
        ("attend", attend),
        ("rejoin", rejoin),
        ("expand", expand),
        ("narrow", narrow),
        ("vin", vin),
    ]
    outputs = [
        ("act", (rows, d_model), pl.ANY),
        ("ing", (rows, d_model), pl.ANY),
        ("ga", (3, vr, hw), pltpu.VMEM),
        ("gr", (vr, hw), pltpu.VMEM),
        ("ge", (vr, uw), pltpu.VMEM),
        ("gn", (vr, uw), pltpu.VMEM),
        ("gv", (vr, LANES), pltpu.VMEM),
        ("norm", (8, LANES), pltpu.VMEM),
    ]
    low = [
        ("wv", (d_model, LANES)),
        ("wa", (3, d_model, hw)),
        ("wr", (d_model, hw)),
        ("we", (d_model, uw)),
        ("wn", (d_model, uw)),
        ("gsv", (d_model, LANES)),
        ("gsa", (3, d_model, hw)),
        ("gsr", (d_model, hw)),
        ("gse", (d_model, uw)),
        ("gsn", (d_model, uw)),
        ("yv", (lines, vr, LANES)),
        ("ya", (lines, 3, vr, hw)),
        ("yr", (lines, vr, hw)),
        ("ye", (lines, vr, uw)),
        ("yn", (lines, vr, uw)),
        ("zv", (ways, vr, LANES)),
        ("za", (ways, 3, vr, hw)),
        ("zr", (ways, vr, hw)),
        ("ze", (ways, vr, uw)),
        ("zn", (ways, vr, uw)),
        ("cs", (2, CHUNKS, ch, d_model)),
        ("cr", (2, CHUNKS, ch, d_model)),
        ("xs", (2, CHUNKS, ch, d_model)),
        ("xr", (2, CHUNKS, ch, d_model)),
        ("vb", (4, vr, LANES)),
        ("oh", (SLOTS, rows)),
        ("oht", (rows, SLOTS)),
        ("mc", (SLOTS, d_model)),
        ("xl", (rows, d_model)),
        ("normed", (rows, d_model)),
        ("low2", (rows, d_model)),
        ("xt", (d_model, 2 * rows)),
        ("nt", (d_model, wide)),
        ("l2t", (d_model, wide)),
        ("l1t", (d_model, wide)),
        ("act0", (wide, uw)),
        ("slope0", (rows, uw)),
        ("be", (wide, uw)),
        ("ctx", (wide, hw)),
        ("ctx1", (rows, hw)),
        ("dp", (3, 2 * rows, hw)),
        ("qz", (2, heads, rows, LANES)),
        ("qzt", (2, heads, LANES, rows)),
        ("kn", (2, rows, hw)),
        ("kt", (2, hw, rows)),
        ("vn", (2, rows, hw)),
        ("vvt", (hw, rows)),
        ("ct", (2, hw, rows)),
        ("p0", (heads, rows, rows)),
        ("doz", (heads, rows, LANES)),
        ("dozt", (heads, LANES, rows)),
        ("dqt", (hw, rows)),
        ("slc", (SLOTS, uw)),
        ("low2c", (SLOTS, d_model)),
        ("slt", (SLOTS, d_model)),
        ("qc", (heads, SLOTS, LANES)),
        ("pc", (heads, rows, SLOTS)),
        ("cct", (hw, SLOTS)),
    ]
    full = [
        ("vt", (16, d_model)),
        ("vg", (16, d_model)),
        ("keep", (rows, 1)),
        ("st", (half, d_model)),
        ("gb", (half, d_model)),
        ("xh1", (2, half, d_model)),
        ("xh2", (2, half, d_model)),
        ("rs1", (2, half, 1)),
        ("rs2", (2, half, 1)),
        ("acc", (ch, d_model)),
        ("part", (SLOTS, TILE)),
        ("vf", (4, vr, LANES)),
        ("ns", (4, 8, LANES)),
        ("nr", (3, 8, LANES)),
        ("nz", (lines, 8, LANES)),
    ]
    sems = [
        ("agzs", (5, lines)),
        ("agzr", (5, lines)),
        ("agys", (5, lines)),
        ("agyr", (5, lines)),
        ("rsys", (5, lines)),
        ("rsyr", (5, lines)),
        ("rszs", (5, lines)),
        ("rszr", (5, lines)),
        ("arcs", (8, CHUNKS)),
        ("arcr", (8, CHUNKS)),
        ("arxs", (8, CHUNKS)),
        ("arxr", (8, CHUNKS)),
        ("shs", (8, CHUNKS)),
        ("shr", (8, CHUNKS)),
        ("vxs", (4,)),
        ("vxr", (4,)),
        ("osem", (8,)),
        ("nss", (3,)),
        ("nsr", (3,)),
        ("nzs", (lines,)),
        ("nzr", (lines,)),
    ]
    names = (
        [name for name, _ in inputs]
        + [name for name, _, _ in outputs]
        + [name for name, _ in low]
        + [name for name, _ in full]
        + ["pb"]
        + [name for name, _ in sems]
    )
    sizes = (n, d_model, rows, hw, uw, vr)

    def body(*refs):
        layer_kernel(names, sizes, *refs)

    return pl.pallas_call(
        body,
        out_shape=[jax.ShapeDtypeStruct(shape, F32) for _, shape, _ in outputs],
        in_specs=[pl.BlockSpec(memory_space=pltpu.VMEM)] * len(inputs),
        out_specs=[pl.BlockSpec(memory_space=space) for _, _, space in outputs],
        scratch_shapes=[pltpu.VMEM(shape, BF) for _, shape in low]
        + [pltpu.VMEM(shape, F32) for _, shape in full]
        + [pltpu.VMEM((16, LANES), jnp.int32)]
        + [pltpu.SemaphoreType.DMA(shape) for _, shape in sems],
        compiler_params=pltpu.CompilerParams(
            collective_id=0, has_side_effects=True, vmem_limit_bytes=61 * 1024 * 1024
        ),
        cost_estimate=pl.CostEstimate(
            flops=20_000_000_000, bytes_accessed=20_000_000, transcendentals=4_000_000
        ),
    )(*[value for _, value in inputs])


def apply_update(weight, first_moment, second_moment, shadow, gradient, step_rate):
    momentum = 0.5 * first_moment + 0.5 * gradient
    variance = 0.5 * second_moment + 0.5 * gradient * gradient
    bias_fix = 1.0 - 0.5**STEP
    updated = weight - step_rate * (
        momentum / bias_fix / (jnp.sqrt(variance / bias_fix) + 1e-08) + 0.01 * weight
    )
    average = 0.999 * shadow + 0.001 * updated
    return (updated, momentum, variance, average, updated.astype(BF))


def per_device(
    tokens_in,
    masked_positions,
    replace_choice,
    replace_table,
    masked_cotangent,
    attend,
    attend_mean,
    attend_square,
    attend_shadow,
    rejoin,
    rejoin_mean,
    rejoin_square,
    rejoin_shadow,
    expand,
    expand_mean,
    expand_square,
    expand_shadow,
    narrow,
    narrow_mean,
    narrow_square,
    narrow_shadow,
    vectors,
    vectors_mean,
    vectors_square,
    vectors_shadow,
):
    n = lax.axis_size("dp")
    m = lax.axis_index("mp")
    vector_rows, vector_width = vectors.shape
    placed_vectors = lax.dynamic_update_slice(
        jnp.zeros((vector_rows, LANES), F32), vectors, (0, m * vector_width)
    )
    act, ing, ga, gr, ge, gn, gv, norm = run_layers(
        n,
        tokens_in,
        masked_positions,
        replace_choice,
        replace_table,
        masked_cotangent,
        attend.transpose(1, 0, 2),
        rejoin,
        expand,
        narrow,
        placed_vectors,
    )
    gradient_norm = norm[0, 0]
    d_model = tokens_in.shape[1]
    param_count = 4 * d_model * d_model + 2 * d_model * expand.shape[1] * 4 + 12 * d_model
    clip_limit = 0.001 * math.sqrt(param_count * tokens_in.shape[0] * n)
    factor = jnp.minimum(1.0, clip_limit / (gradient_norm + 1e-06))
    gv = lax.dynamic_slice(gv, (0, m * vector_width), (vector_rows, vector_width))
    results = [act, ing, gradient_norm]
    for group in (
        (attend, attend_mean, attend_square, attend_shadow, ga.transpose(1, 0, 2), 0.04),
        (rejoin, rejoin_mean, rejoin_square, rejoin_shadow, gr, 0.16),
        (expand, expand_mean, expand_square, expand_shadow, ge, 0.04),
        (narrow, narrow_mean, narrow_square, narrow_shadow, gn, 0.04),
        (vectors, vectors_mean, vectors_square, vectors_shadow, gv, 0.5),
    ):
        results.extend(apply_update(*group[:4], group[4] * factor, group[5]))
    return tuple(results)


def solution(mesh):
    row = P("dp", None)
    cube = P("dp", None, "mp")
    flat = P("dp", "mp")
    return jax.shard_map(
        per_device,
        mesh=mesh,
        in_specs=(row, row, row, P(), P("dp", None, None)) + (cube,) * 4 + (flat,) * 16,
        out_specs=(row, row, P()) + (cube,) * 5 + (flat,) * 20,
        check_vma=False,
    )
```

time: 981 us -> 325 us (0.33)
  waiting for transfers between devices: 606 us -> 0 us
  Pallas kernels: 0 us -> 300 us
  blocking collectives: 159 us -> 0 us
  matrix products: 85.3 us -> 0 us
  other arithmetic: 57 us -> 11.3 us
  local copies, waits for them, and re-layouts: 33.2 us -> 11.9 us
  between operations: 20.6 us -> 1.6 us
  starting transfers between devices: 11.7 us -> 0 us
    pallas_call x0 -> x1, Pallas kernels: none -> 300 us  [run_layers(): pl.pallas_call(body, out_shape=[jax.ShapeDtypeStruct(shape, F32) for _, s...]
    reduce_scatter x4 -> x0, waiting for transfers between devices: 272 us -> none  [the longest x1 88.9 us: per_device(): lax.psum_scatter(matrix_back[3], 'dp', scatter_dimension=0, tiled=True)]
    psum x8 -> x0, waiting for transfers between devices: 238 us -> none  [the longest x2 72.6 us: backward_step(): lax.psum(over_columns(back_expanded, expand_full).astype(jnp.bfloat16), '...]
    all_gather x3 -> x0, waiting for transfers between devices: 96.3 us -> none  [the longest x1 50 us: per_device(): lax.all_gather(low_expand, 'dp', axis=0, tiled=True)]
    dot_general x36 -> x0, matrix products: 77.3 us -> none  [the longest x8 28.3 us: over_rows(): lax.dot_general(former, latter, (((0,), (0,)), ((), ())), preferred_eleme...]
    all_gather x2 -> x0, blocking collectives: 74.9 us -> none  [the longest x1 43.7 us: per_device(): lax.all_gather(vectors.astype(jnp.bfloat16).reshape(1, vector_rows * vect...]
    unnamed x1 -> x0, blocking collectives: 43.5 us -> none
    psum x1 -> x0, blocking collectives: 40.6 us -> none  [per_device(): gradient_norm = jnp.sqrt(lax.psum(local_squares, ('dp', 'mp')))]
  transfers between devices with their start and end apart: 15 -> 0, of which waited for: 13 -> 0; matrix products, arithmetic and copies ran while one was open for 6% -> 0% of each run, Pallas kernels for 0% -> 0%
where the time goes in v1:
time: 325 us
  Pallas kernels  300 us (92%)
  local copies, waits for them, and re-layouts  11.9 us (4%)
  other arithmetic  11.3 us (3%)
    pallas_call x1, Pallas kernels, run_layers(): pl.pallas_call(body, out_shape=[jax.ShapeDtypeStruct(shape, F32) for _, s...  300 us
    unnamed x62, local copies, waits for them, and re-layouts  9.6 us

profile of v1, /device:TPU:0, one launch (start us, length us, event | category | flops | bytes accessed | tf_op | source)
XLA Modules:
  0.0 324.6 jit_solution(12920996554313386797)
XLA Ops:
  0.7 0.7 broadcast_multiply_fusion.3
  1.4 0.7 broadcast_multiply_fusion.2
  2.0 0.7 broadcast_multiply_fusion.1
  3.1 0.8 copy.71
  4.3 0.6 copy-done.25
  4.9 299.8 %shard_map.456 = (f32[512,1024]{1,0:T(8,128)}, f32[512,1024]{1,0:T(8,128)}, f32[3,128,256]{2,1,0:T(8,128)}, f32[128,256]{1,0:T(8,128)}, f32[128,1024]{1,0:T(8,12...) custom-call(bf16[512,1024]{1,0:T(8,128)(2,1)} %refs_0_.1, s32[1,96]{1,0:T(1,128)} %refs_1_.1, ...), custom_call_target="tpu_custom_call" | custom-call | flops 20000000000 | bytes 20000000 | tf_op jit(solution)/shard_map/pallas_call | solution.py:1020
  304.8 1.3 slice.3
  306.8 1.0 sqrt_add_fusion
  307.8 0.7 copy.82
  308.6 0.7 copy.81
  309.4 0.7 copy.84
  310.0 0.7 copy.80
  310.7 0.7 copy.83
  311.4 1.7 fusion.11
  313.1 0.7 multiply_add_fusion.7
  313.9 1.2 fusion.13
  315.0 0.8 multiply_add_fusion.5
  316.5 2.1 fusion.7
  318.6 0.9 multiply_add_fusion.3
  319.5 0.9 multiply_add_fusion.4
  320.4 0.6 copy-done.3
  320.9 1.3 copy.88
  322.2 1.0 copy-done.2
  323.3 1.3 copy.89
  (62 shorter events, 1.7 us)
Async XLA Ops:
  4.9 303.6 %copy-start.26 = (f32[128,3]{0,1:T(4,128)S(1)}, f32[128,3]{0,1:T(4,128)}, u32[]{:S(2)}) copy-start(f32[128,3]{0,1:T(4,128)} %param.46) | copy-start | bytes 4612
  4.9 306.4 %copy-start.21 = (f32[128,256]{1,0:T(8,128)S(1)}, f32[128,256]{1,0:T(8,128)}, u32[]{:S(2)}) copy-start(f32[128,256]{1,0:T(8,128)} %refs_6_.1) | copy-start | bytes 393220
  4.9 306.4 %copy-start.22 = (f32[128,256]{1,0:T(8,128)S(1)}, f32[128,256]{1,0:T(8,128)}, u32[]{:S(2)}) copy-start(f32[128,256]{1,0:T(8,128)} %param.35) | copy-start | bytes 393220
  4.9 306.4 %copy-start.23 = (f32[128,256]{1,0:T(8,128)S(1)}, f32[128,256]{1,0:T(8,128)}, u32[]{:S(2)}) copy-start(f32[128,256]{1,0:T(8,128)} %param.36) | copy-start | bytes 393220
  304.7 8.3 %copy-start.24 = (f32[128,256]{1,0:T(8,128)S(1)}, f32[128,256]{1,0:T(8,128)}, u32[]{:S(2)}) copy-start(f32[128,256]{1,0:T(8,128)} %param.37) | copy-start | bytes 393220
  304.8 9.0 %copy-start.16 = (f32[128,3,256]{2,0,1:T(8,128)S(1)}, f32[128,3,256]{2,0,1:T(8,128)}, u32[]{:S(2)}) copy-start(f32[128,3,256]{2,0,1:T(8,128)} %param.30) | copy-start | bytes 1179652
  304.8 9.0 %copy-start.17 = (f32[128,3,256]{2,0,1:T(8,128)S(1)}, f32[128,3,256]{2,0,1:T(8,128)}, u32[]{:S(2)}) copy-start(f32[128,3,256]{2,0,1:T(8,128)} %param.31) | copy-start | bytes 1179652
  304.8 9.0 %copy-start.18 = (f32[128,3,256]{2,0,1:T(8,128)S(1)}, f32[128,3,256]{2,0,1:T(8,128)}, u32[]{:S(2)}) copy-start(f32[128,3,256]{2,0,1:T(8,128)} %param.32) | copy-start | bytes 1179652
  304.8 9.0 %copy-start.19 = (f32[3,128,256]{2,1,0:T(8,128)S(1)}, f32[3,128,256]{2,1,0:T(8,128)}, u32[]{:S(2)}) copy-start(f32[3,128,256]{2,1,0:T(8,128)} %get-tuple-element.39) | copy-start | bytes 1179652
  311.3 3.7 %copy-start.20 = (f32[128,3,256]{2,0,1:T(8,128)S(1)}, f32[128,3,256]{2,0,1:T(8,128)}, u32[]{:S(2)}) copy-start(f32[128,3,256]{2,0,1:T(8,128)} %param.33) | copy-start | bytes 1179652
  313.1 2.8 copy-start.15
  313.1 2.8 copy-start.14
  313.8 2.1 copy-start.5
  313.8 2.1 copy-start.6
  313.8 2.1 copy-start.7
  313.8 2.3 copy-start.10
  313.9 2.6 copy-start.13
  315.0 3.5 %copy-start.4 = (f32[128,3,256]{2,0,1:T(8,128)}, f32[128,3,256]{2,0,1:T(8,128)S(1)}, u32[]{:S(2)}) copy-start(f32[128,3,256]{2,0,1:T(8,128)S(1)} %get-tuple-element.159) | copy-start | bytes 1179652
  316.5 2.1 copy-start.11
  316.5 3.0 copy-start.12
  318.6 3.7 %copy-start = (f32[128,1024]{1,0:T(8,128)}, f32[128,1024]{1,0:T(8,128)S(1)}, u32[]{:S(2)}) copy-start(f32[128,1024]{1,0:T(8,128)S(1)} %get-tuple-element.174) | copy-start | bytes 1572868
  318.6 3.7 %copy-start.1 = (f32[128,1024]{1,0:T(8,128)}, f32[128,1024]{1,0:T(8,128)S(1)}, u32[]{:S(2)}) copy-start(f32[128,1024]{1,0:T(8,128)S(1)} %get-tuple-element.169) | copy-start | bytes 1572868
  318.6 2.3 copy-start.3
  320.9 2.3 copy-start.2
  (3 other events, 4.7 us)

commit v2 on v1

--- a/solution.py
+++ b/solution.py
@@ -79,6 +79,7 @@
     core_peer = (d, m + 1 - 2 * core)
     x_peer = (d, (m + 2) % 4)
     y_peer = (d + 1 - 2 * y, m)
+    model_peers = (core_peer, x_peer, (d, 3 - m))
     own0 = core * half
     oth0 = half - own0
 
@@ -89,6 +90,9 @@
 
     def z_peer(step):
         return (((z + step) % lines) * 2 + y, m)
+
+    def zy_peer(step):
+        return (((z + step) % lines) * 2 + 1 - y, m)
 
     def z_from(step):
         return ((z + lines - step) % lines) * 2 + y
@@ -108,14 +112,15 @@
         )
 
     barrier = pltpu.get_barrier_semaphore()
-    for peer in (core_peer, x_peer, y_peer):
+
+    def greet(peer):
         pl.semaphore_signal(barrier, inc=1, device_id=peer, device_id_type=MESH)
-    each(
-        1,
-        lines,
-        lambda s: pl.semaphore_signal(barrier, inc=1, device_id=z_peer(s), device_id_type=MESH),
-    )
-    pl.semaphore_wait(barrier, 3 + lines - 1)
+
+    for peer in model_peers:
+        greet(peer)
+    each(1, lines, lambda s: greet(z_peer(s)))
+    each(0, lines, lambda s: greet(zy_peer(s)))
+    pl.semaphore_wait(barrier, len(model_peers) + n - 1)
 
     def gather_z(region, step):
         piece = block(weights[region], region, d)
@@ -141,12 +146,15 @@
         each(1, lines, lambda s: gather_z(region, s).start())
         gather_y(region, 0).start()
 
-    def gather_pass(region):
+    def gather_pass(region, only=None):
         def one(step):
             gather_z_arrival(region, step).wait_recv()
             gather_y(region, step).start()
 
-        each(1, lines, one)
+        if only is None:
+            each(1, lines, one)
+        else:
+            one(only)
 
     def gather_wait(region):
         each(0, lines, lambda s: gather_y_arrival(region, s).wait_recv())
@@ -269,7 +277,10 @@
         ref[aligned(oth0 + q * ch, ch), cols] = value[:ch]
         ref[aligned(own0 + q * ch, ch), cols] = value[ch:]
 
-    r.vb[0] = r.vin[...].astype(BF)
+    columns = r.vin.shape[0]
+    r.vs[...] = jnp.zeros(r.vs.shape, F32)
+    r.vs[pl.ds(columns * m, columns), :] = r.vin[...]
+    r.vb[0] = low_transpose(r.vs[...])
     swap = remote(r.vb.at[0], r.vb.at[1], r.vxs.at[0], r.vxr.at[0], core_peer)
     swap.start()
     mine = aligned(d * vr, vr)
@@ -372,12 +383,19 @@
     for ref in (r.qzt, r.dozt):
         ref[...] = jnp.zeros(ref.shape, BF)
 
-    def share_block(layer, head, lane0):
+    def share_block(layer, head, lane0, width):
         if layer == 0:
-            return r.p0.at[head, :, aligned(lane0, TILE)]
+            return r.p0.at[head, :, aligned(lane0, width)]
         return r.gse.at[
-            aligned((head // 2) * rows, rows), aligned((head % 2) * rows + lane0, TILE)
+            (head // 2) * rows : (head // 2 + 1) * rows,
+            aligned((head % 2) * rows + lane0, width),
         ]
+
+    def both_lanes(ref, where, q):
+        return jnp.concatenate(
+            [ref[where, aligned(oth0 + q * ch, ch)], ref[where, aligned(own0 + q * ch, ch)]],
+            axis=1,
+        )
 
     def project(layer, q):
         x = both(r.xl, q)
@@ -391,25 +409,22 @@
         put_both(r.vn.at[layer], q, slice(None), values)
         put_across(r.vvt, q, low_transpose(values))
 
-    def attend_forward(layer):
-        def one(i):
-            head, lane0 = i // 2, (i % 2) * TILE
-            pair = aligned((head // 2) * LANES, LANES)
-            lanes = aligned(lane0, TILE)
-            scores = nn(r.kn[layer, :, pair], r.qzt[layer, head, :, lanes])
+    def attend_forward(layer, q):
+        for head in range(heads):
+            pair = slice((head // 2) * LANES, (head // 2 + 1) * LANES)
+            across = both_lanes(r.qzt.at[layer, head], slice(None), q)
+            scores = nn(r.kn[layer, :, pair], across)
             raised = jnp.exp(scores - jnp.max(scores, axis=0, keepdims=True))
             total = jnp.sum(raised, axis=0, keepdims=True)
             low = (raised * (1.0 / total)).astype(BF)
-            share_block(layer, head, lane0)[...] = low
-            where = aligned(head * HEAD_DIM, HEAD_DIM)
-            r.ct[layer, where, lanes] = nn(r.vvt[where, :], low).astype(BF)
-
-        loop(heads * (rows // TILE), one)
-        target, row0 = (r.ctx, 0) if layer == 0 else (r.ctx1, 0)
-        for i in range(rows // LANES):
-            target[row0 + i * LANES : row0 + (i + 1) * LANES, :] = low_transpose(
-                r.ct[layer, :, i * LANES : (i + 1) * LANES]
-            )
+            share_block(layer, head, oth0 + q * ch, ch)[...] = low[:, :ch]
+            share_block(layer, head, own0 + q * ch, ch)[...] = low[:, ch:]
+            where = slice(head * HEAD_DIM, (head + 1) * HEAD_DIM)
+            context = nn(r.vvt[where, :], low).astype(BF)
+            r.ct[layer, where, aligned(oth0 + q * ch, ch)] = context[:, :ch]
+            r.ct[layer, where, aligned(own0 + q * ch, ch)] = context[:, ch:]
+        target = r.ctx if layer == 0 else r.ctx1
+        put_both(target, q, slice(None), low_transpose(both_lanes(r.ct.at[layer], slice(None), q)))
 
     def first_norm(layer, q):
         def one(i):
@@ -476,6 +491,50 @@
         act = unit_act(layer)
         sum_begin(2 * layer + 1, q, lambda cols: nt(both(act, q), r.wn[cols, :]), ch)
 
+    hot = r.oh[...]
+
+    def pick(target, row0, source, source0, width):
+        def one(j):
+            cols = aligned(j * TILE, TILE)
+            target[row0 : row0 + SLOTS, cols] = nn(
+                hot, source[source0 : source0 + rows, cols]
+            ).astype(BF)
+
+        loop(width // TILE, one)
+
+    by_columns = (2 * vr) % LANES == 0
+
+    def column_core(step):
+        cols = aligned((z_from(step) - y) * vr, 2 * vr)
+        return remote(
+            r.cs.at[1, :, :, cols],
+            r.cr.at[1, :, :, cols],
+            r.ccs.at[step],
+            r.ccr.at[step],
+            core_peer,
+        )
+
+    def column_x(step):
+        cols = aligned((z_from(step) - y) * vr, 2 * vr)
+        return remote(
+            r.xs.at[1, :, :, cols], r.xr.at[1, :, :, cols], r.cxs.at[step], r.cxr.at[step], x_peer
+        )
+
+    def column_sum(step):
+        cols = aligned((z_from(step) - y) * vr, 2 * vr)
+        weight = r.wn[cols, :]
+        away = nt(r.act0[aligned(oth0, half), :], weight).astype(BF)
+        for q in range(CHUNKS):
+            r.cs[1, q, :, cols] = away[q * ch : (q + 1) * ch]
+        column_core(step).start()
+        here = nt(r.act0[aligned(own0, half), :], weight)
+        column_core(step).wait_recv()
+        for q in range(CHUNKS):
+            r.xs[1, q, :, cols] = (
+                here[q * ch : (q + 1) * ch] + r.cr[1, q, :, cols].astype(F32)
+            ).astype(BF)
+        column_x(step).start()
+
     for layer in range(DEPTH):
         for q in range(CHUNKS):
             if layer > 0:
@@ -483,10 +542,10 @@
             project(layer, q)
         if layer == 0:
             gather_pass(REJ)
-        attend_forward(layer)
-        if layer == 0:
-            gather_wait(REJ)
         for q in range(CHUNKS):
+            attend_forward(layer, q)
+            if layer == 0 and q == 0:
+                gather_wait(REJ)
             rejoin_sum(layer, q)
         if layer == 0:
             gather_start(NAR)
@@ -501,17 +560,45 @@
                 gather_wait(EXP)
             share_wait(2 * layer, r.normed, q)
             widen(layer, q)
-            if layer == 0 and q == 0:
+            if layer > 0:
+                narrow_sum(layer, q)
+        if layer == 0:
+            transpose_into(r.nt, 0, r.normed, 0, rows)
+            if by_columns:
+                for step in range(lines):
+                    if step < lines - 1:
+                        gather_pass(NAR, step + 1)
+                    gather_y_arrival(NAR, step).wait_recv()
+                    column_sum(step)
+                for step in range(lines):
+                    column_x(step).wait()
+                    column_core(step).wait_send()
+            else:
                 gather_pass(NAR)
                 gather_wait(NAR)
-            narrow_sum(layer, q)
-        if layer == 0:
-            transpose_into(r.nt, 0, r.normed, 0, rows)
+                for q in range(CHUNKS):
+                    narrow_sum(layer, q)
+        else:
+            pick(r.act0, rows, r.gsn, 0, uw)
+            pick(r.slc, 0, r.gsn, rows, uw)
+            for head in range(heads):
+                r.qc[head] = nn(hot, r.qz[1, head]).astype(BF)
+                source = r.gse[
+                    (head // 2) * rows : (head // 2 + 1) * rows,
+                    (head % 2) * rows : (head % 2 + 1) * rows,
+                ]
+                r.pc[head] = nn(source, r.oht[...]).astype(BF)
         for q in range(CHUNKS):
-            sum_end(2 * layer + 1, q, ch)
+            if not (layer == 0 and by_columns):
+                sum_end(2 * layer + 1, q, ch)
             second_norm(layer, q)
             if layer < DEPTH - 1:
                 share(2 * layer + 1, r.xl, q).start()
+            elif q == 0:
+                pick(r.low2c, 0, r.normed, 0, d_model)
+                transpose_into(r.nt, rows, r.low2c, 0, SLOTS)
+                pick(r.ctx, rows, r.ctx1, 0, hw)
+                r.cct[...] = nn(r.ct[1], r.oht[...]).astype(BF)
 
     own_rows = aligned(own0, half)
     out_here = pltpu.make_async_copy(r.st, r.act.at[own_rows], r.osem.at[0])
@@ -572,22 +659,6 @@
     for q in range(CHUNKS):
         second_pull(1, q, lambda i, at: nn(hot_rows(q * ch + i * SUB), r.mc[...]))
         share(4, r.low2, q).start()
-    hot = r.oh[...]
-
-    def pick(target, row0, source, source0, width):
-        def one(j):
-            cols = aligned(j * TILE, TILE)
-            target[row0 : row0 + SLOTS, cols] = nn(
-                hot, source[source0 : source0 + rows, cols]
-            ).astype(BF)
-
-        loop(width // TILE, one)
-
-    pick(r.act0, rows, r.gsn, 0, uw)
-    pick(r.slc, 0, r.gsn, rows, uw)
-    pick(r.low2c, 0, r.normed, 0, d_model)
-    transpose_into(r.nt, rows, r.low2c, 0, SLOTS)
-    pick(r.ctx, rows, r.ctx1, 0, hw)
     for q in range(CHUNKS):
         share_wait(4, r.low2, q)
     pick(r.low2c, 0, r.low2, 0, d_model)
@@ -630,14 +701,6 @@
         )
         share(5, r.xl, q).start()
 
-    for head in range(heads):
-        r.qc[head] = nn(hot, r.qz[1, head]).astype(BF)
-        source = r.gse[
-            (head // 2) * rows : (head // 2 + 1) * rows,
-            (head % 2) * rows : (head % 2 + 1) * rows,
-        ]
-        r.pc[head] = nn(source, r.oht[...]).astype(BF)
-    r.cct[...] = nn(r.ct[1], r.oht[...]).astype(BF)
     for q in range(CHUNKS):
         share_wait(5, r.xl, q)
     pick(r.low2c, 0, r.xl, 0, d_model)
@@ -688,6 +751,25 @@
     for q in range(CHUNKS):
         layer_rows(5, q, rows)
 
+    def weight_grad_rows(target, across, latter, width, row0, count):
+        at = aligned(row0, count)
+
+        def one(j):
+            cols = aligned(j * TILE, TILE)
+            target[at, cols] = nn(across[at, :], latter[:, cols]).astype(BF)
+
+        loop(width // TILE, one)
+
+    def weight_grad(target, across, latter, width):
+        loop(
+            d_model // TILE,
+            lambda i: weight_grad_rows(target, across, latter, width, i * TILE, TILE),
+        )
+
+    def transpose_both(target, source, q):
+        for row0 in (oth0 + q * ch, own0 + q * ch):
+            target[:, aligned(row0, ch)] = low_transpose(source[aligned(row0, ch), :])
+
     for q in range(CHUNKS):
         sum_end(5, q, ch)
         second_pull(
@@ -695,6 +777,20 @@
         )
         share(6, r.low2, q).start()
         share_wait(6, r.low2, q)
+        transpose_both(r.l2t, r.low2, q)
+        if q == CHUNKS - 1:
+            if by_columns:
+
+                def first_rows(step):
+                    owner = ((z + step) % lines) * 2 + 1 - y
+                    weight_grad_rows(r.gsn, r.l2t, r.act0, uw, owner * vr, vr)
+                    scatter_y(NAR, step).start()
+
+                each(1, lines, first_rows)
+                first_rows(0)
+            else:
+                weight_grad(r.gsn, r.l2t, r.act0, uw)
+                scatter_start(NAR)
 
         def units(j, q=q):
             cols = aligned(j * TILE, TILE)
@@ -706,26 +802,31 @@
         loop(uw // TILE, units)
         sum_begin(6, q, lambda cols, q=q: nt(both(r.be, q), r.we[cols, :]), ch)
 
-    def weight_grad(target, across, latter, width):
-        def one(t):
-            i, j = t // (width // TILE), t % (width // TILE)
-            at, cols = aligned(i * TILE, TILE), aligned(j * TILE, TILE)
-            target[at, cols] = nn(across[at, :], latter[:, cols]).astype(BF)
-
-        loop((d_model // TILE) * (width // TILE), one)
-
-    transpose_into(r.l2t, 0, r.low2, 0, rows)
-    weight_grad(r.gsn, r.l2t, r.act0, uw)
-    scatter_start(NAR)
+    if by_columns:
+        each(
+            0,
+            lines,
+            lambda s: weight_grad_rows(
+                r.gsn, r.l2t, r.act0, uw, (((z + s) % lines) * 2 + y) * vr, vr
+            ),
+        )
     weight_grad(r.gse, r.nt, r.be, uw)
     scatter_start(EXP)
+    passes = [lambda s=s: scatter_pass(NAR, s) for s in range(1, lines)]
+    passes += [lambda s=s: scatter_pass(EXP, s) for s in range(1, lines)]
+
+    def pump(count=1):
+        for _ in range(min(count, len(passes))):
+            passes.pop(0)()
+
+    pump()
     for q in range(CHUNKS):
         sum_end(6, q, ch)
         first_pull(
             0, q, lambda i, at: r.gb[at, :] + sum_rows(6, q, aligned(i * SUB, SUB))
         )
         share(7, r.xl, q).start()
-    scatter_pass(NAR, 1) if lines > 1 else None
+    pump()
     for q in range(CHUNKS):
         share_wait(7, r.xl, q)
         back = nn(both(r.xl, q), r.wr[...]).astype(BF)
@@ -760,6 +861,7 @@
         r.dp[0, some, :] = low_transpose(r.dqt[:, some])
     for q in range(CHUNKS):
         layer_rows(7, q, 0)
+    pump()
     bias_sums(0)
     transpose_into(r.l1t, 0, r.xl, 0, rows)
     weight_grad(r.gsr, r.l1t, r.ctx, hw)
@@ -775,7 +877,7 @@
     for kind in range(3):
         weight_grad(r.gsa.at[kind], r.xt, r.dp.at[kind], hw)
     scatter_start(ATT)
-    each(2, lines, lambda s: scatter_pass(NAR, s))
+    pump()
     out_here.wait()
     out_there.wait_send()
     for q in range(CHUNKS):
@@ -793,7 +895,7 @@
     in_here.start()
     in_there.start()
 
-    each(1, lines, lambda s: scatter_pass(EXP, s))
+    pump(len(passes))
     each(1, lines, lambda s: scatter_pass(REJ, s))
     each(1, lines, lambda s: scatter_pass(VEC, s))
     each(1, lines, lambda s: scatter_pass(ATT, s))
@@ -817,44 +919,41 @@
     swap_w = remote(r.vf.at[2], r.vf.at[3], r.vxs.at[3], r.vxr.at[3], x_peer)
     swap_w.start()
     swap_w.wait_recv()
-    r.gv[...] = r.vf[2] + r.vf[3]
-    lane = lax.broadcasted_iota(jnp.int32, r.gv.shape, 1)
-    own_lanes = jnp.logical_and(lane >= 3 * m, lane < 3 * m + 3)
-    total = total + squares(jnp.where(own_lanes, r.gv[...], 0.0))
+    r.vs[...] = jnp.transpose(r.vf[2] + r.vf[3], (1, 0))
+    r.gv[...] = r.vs[pl.ds(columns * m, columns), :]
+    total = total + squares(r.gv[...])
     scatter_finish(ATT, r.ga)
     total = total + squares(r.ga[...])
 
-    r.ns[0] = jnp.broadcast_to(total, (8, LANES))
-    for step, peer in enumerate((core_peer, x_peer, y_peer)):
-        swap_n = remote(r.ns.at[step], r.nr.at[step], r.nss.at[step], r.nsr.at[step], peer)
-        swap_n.start()
-        swap_n.wait_recv()
-        r.ns[step + 1] = r.ns[step] + r.nr[step]
-    r.nz[z] = r.ns[3]
-
-    def norm_copy(step):
-        return remote(
-            r.ns.at[3], r.nz.at[z], r.nzs.at[step], r.nzr.at[step], z_peer(step)
-        )
-
-    def norm_arrival(step):
-        return remote(
-            r.ns.at[3],
-            r.nz.at[(z + lines - step) % lines],
-            r.nzs.at[step],
-            r.nzr.at[step],
-            z_peer(step),
-        )
-
-    each(1, lines, lambda s: norm_copy(s).start())
-    each(1, lines, lambda s: norm_arrival(s).wait_recv())
+    r.nm[m] = jnp.broadcast_to(total, (8, LANES))
+
+    def model_copy(k, slot):
+        return remote(r.nm.at[slot], r.nm.at[slot], r.nms.at[k], r.nmr.at[k], model_peers[k])
+
+    for k in range(3):
+        model_copy(k, m).start()
+    for k in range(3):
+        model_copy(k, model_peers[k][1]).wait_recv()
+    r.nz[d] = jnp.sum(r.nm[...], axis=0)
+
+    def line_copy(step, slot):
+        here = r.nz.at[slot]
+        return remote(here, here, r.nzs.at[0, step], r.nzr.at[0, step], z_peer(step))
+
+    def cross_copy(step, slot):
+        here = r.nz.at[slot]
+        return remote(here, here, r.nzs.at[1, step], r.nzr.at[1, step], zy_peer(step))
+
+    each(0, lines, lambda s: cross_copy(s, d).start())
+    each(1, lines, lambda s: line_copy(s, d).start())
+    each(0, lines, lambda s: cross_copy(s, z_from(s) + 1 - 2 * y).wait_recv())
+    each(1, lines, lambda s: line_copy(s, z_from(s)).wait_recv())
     r.norm[...] = jnp.sqrt(jnp.sum(r.nz[...], axis=0))
 
-    each(1, lines, lambda s: norm_copy(s).wait_send())
-    for step, peer in enumerate((core_peer, x_peer, y_peer)):
-        remote(
-            r.ns.at[step], r.nr.at[step], r.nss.at[step], r.nsr.at[step], peer
-        ).wait_send()
+    each(0, lines, lambda s: cross_copy(s, d).wait_send())
+    each(1, lines, lambda s: line_copy(s, d).wait_send())
+    for k in range(3):
+        model_copy(k, m).wait_send()
     swap.wait_send()
     swap_x.wait_send()
     swap_v.wait_send()
@@ -901,7 +1000,7 @@
         ("gr", (vr, hw), pltpu.VMEM),
         ("ge", (vr, uw), pltpu.VMEM),
         ("gn", (vr, uw), pltpu.VMEM),
-        ("gv", (vr, LANES), pltpu.VMEM),
+        ("gv", vin.shape, pltpu.VMEM),
         ("norm", (8, LANES), pltpu.VMEM),
     ]
     low = [
@@ -977,9 +1076,9 @@
         ("acc", (ch, d_model)),
         ("part", (SLOTS, TILE)),
         ("vf", (4, vr, LANES)),
-        ("ns", (4, 8, LANES)),
-        ("nr", (3, 8, LANES)),
-        ("nz", (lines, 8, LANES)),
+        ("vs", (LANES, vr)),
+        ("nm", (4, 8, LANES)),
+        ("nz", (n, 8, LANES)),
     ]
     sems = [
         ("agzs", (5, lines)),
@@ -999,10 +1098,14 @@
         ("vxs", (4,)),
         ("vxr", (4,)),
         ("osem", (8,)),
-        ("nss", (3,)),
-        ("nsr", (3,)),
-        ("nzs", (lines,)),
-        ("nzr", (lines,)),
+        ("nms", (3,)),
+        ("nmr", (3,)),
+        ("nzs", (2, lines)),
+        ("nzr", (2, lines)),
+        ("ccs", (lines,)),
+        ("ccr", (lines,)),
+        ("cxs", (lines,)),
+        ("cxr", (lines,)),
     ]
     names = (
         [name for name, _ in inputs]
@@ -1044,6 +1147,71 @@
     )
     average = 0.999 * shadow + 0.001 * updated
     return (updated, momentum, variance, average, updated.astype(BF))
+
+
+def update_kernel(rates, clip_limit, norm, act, ing, *refs):
+    *refs, norm_out, act_out, ing_out = refs
+    act_out[...] = act[...]
+    ing_out[...] = ing[...]
+    norm_out[...] = norm[0:1, 0:1]
+    factor = jnp.minimum(1.0, clip_limit / (norm[0:1, 0:1] + 1e-06))
+    ins, outs = refs[: 5 * len(rates)], refs[5 * len(rates) :]
+    for index, rate in enumerate(rates):
+        weight, first, second, shadow, gradient = ins[5 * index : 5 * index + 5]
+        targets = outs[5 * index : 5 * index + 5]
+        for part in range(weight.shape[0]) if len(weight.shape) == 3 else (slice(None),):
+            results = apply_update(
+                weight[part],
+                first[part],
+                second[part],
+                shadow[part],
+                gradient[part] * factor,
+                rate,
+            )
+            for target, value in zip(targets, results, strict=True):
+                target[part] = value
+
+
+def run_update(groups, rates, norm, clip_limit, act, ing):
+    vr = groups[1][0].shape[0]
+    step = min(vr, 32)
+
+    def spec(shape, whole):
+        if whole:
+            return pl.BlockSpec(shape, lambda i: (0, 0))
+        if len(shape) == 3:
+            return pl.BlockSpec((shape[0], step, shape[2]), lambda i: (0, i, 0))
+        return pl.BlockSpec((step, shape[1]), lambda i: (i, 0))
+
+    last = len(groups) - 1
+    passed = pl.BlockSpec((act.shape[0] * step // vr, act.shape[1]), lambda i: (i, 0))
+    specs = [spec(group[0].shape, k == last) for k, group in enumerate(groups)]
+
+    def body(*refs):
+        update_kernel(rates, clip_limit, *refs)
+
+    flat = [value for group in groups for value in group]
+    size = sum(value.size for value in flat) * 4
+    outs = pl.pallas_call(
+        body,
+        grid=(vr // step,),
+        in_specs=[spec(norm.shape, True)]
+        + [passed] * 2
+        + [one for one in specs for _ in range(5)],
+        out_specs=[one for one in specs for _ in range(5)]
+        + [spec((1, 1), True)]
+        + [passed] * 2,
+        out_shape=[
+            jax.ShapeDtypeStruct(group[0].shape, kind)
+            for group in groups
+            for kind in (F32, F32, F32, F32, BF)
+        ]
+        + [jax.ShapeDtypeStruct(shape, F32) for shape in ((1, 1), act.shape, ing.shape)],
+        compiler_params=pltpu.CompilerParams(vmem_limit_bytes=60 * 1024 * 1024),
+        cost_estimate=pl.CostEstimate(flops=size, bytes_accessed=2 * size, transcendentals=0),
+    )(norm, act, ing, *flat)
+    groups_out = [outs[5 * k : 5 * k + 5] for k in range(len(groups))]
+    return groups_out, outs[-3].reshape(()), *outs[-2:]
 
 
 def per_device(
@@ -1074,11 +1242,6 @@
     vectors_shadow,
 ):
     n = lax.axis_size("dp")
-    m = lax.axis_index("mp")
-    vector_rows, vector_width = vectors.shape
-    placed_vectors = lax.dynamic_update_slice(
-        jnp.zeros((vector_rows, LANES), F32), vectors, (0, m * vector_width)
-    )
     act, ing, ga, gr, ge, gn, gv, norm = run_layers(
         n,
         tokens_in,
@@ -1090,23 +1253,32 @@
         rejoin,
         expand,
         narrow,
-        placed_vectors,
+        vectors.T,
     )
-    gradient_norm = norm[0, 0]
     d_model = tokens_in.shape[1]
     param_count = 4 * d_model * d_model + 2 * d_model * expand.shape[1] * 4 + 12 * d_model
     clip_limit = 0.001 * math.sqrt(param_count * tokens_in.shape[0] * n)
-    factor = jnp.minimum(1.0, clip_limit / (gradient_norm + 1e-06))
-    gv = lax.dynamic_slice(gv, (0, m * vector_width), (vector_rows, vector_width))
+    cubes = [x.transpose(1, 0, 2) for x in (attend, attend_mean, attend_square, attend_shadow)]
+    rows_of = [x.T for x in (vectors, vectors_mean, vectors_square, vectors_shadow)]
+    new, gradient_norm, act, ing = run_update(
+        (
+            (*cubes, ga),
+            (rejoin, rejoin_mean, rejoin_square, rejoin_shadow, gr),
+            (expand, expand_mean, expand_square, expand_shadow, ge),
+            (narrow, narrow_mean, narrow_square, narrow_shadow, gn),
+            (*rows_of, gv),
+        ),
+        (0.04, 0.16, 0.04, 0.04, 0.5),
+        norm,
+        clip_limit,
+        act,
+        ing,
+    )
     results = [act, ing, gradient_norm]
-    for group in (
-        (attend, attend_mean, attend_square, attend_shadow, ga.transpose(1, 0, 2), 0.04),
-        (rejoin, rejoin_mean, rejoin_square, rejoin_shadow, gr, 0.16),
-        (expand, expand_mean, expand_square, expand_shadow, ge, 0.04),
-        (narrow, narrow_mean, narrow_square, narrow_shadow, gn, 0.04),
-        (vectors, vectors_mean, vectors_square, vectors_shadow, gv, 0.5),
-    ):
-        results.extend(apply_update(*group[:4], group[4] * factor, group[5]))
+    results.extend(x.transpose(1, 0, 2) for x in new[0])
+    for group in new[1:4]:
+        results.extend(group)
+    results.extend(x.T for x in new[4])
     return tuple(results)
 
 

time: 325 us -> 293 us (0.902)
  local copies, waits for them, and re-layouts: 11.9 us -> 0 us
  other arithmetic: 11.3 us -> 0 us
  Pallas kernels: 300 us -> 292 us
    pallas_call x1, Pallas kernels: 300 us -> 282 us  [run_layers(): pl.pallas_call(body, out_shape=[jax.ShapeDtypeStruct(shape, F32) for _, s...]
    unnamed x62 -> x0, local copies, waits for them, and re-layouts: 9.6 us -> none
    pallas_call x0 -> x1, Pallas kernels: none -> 9.52 us  [run_update(): pl.pallas_call(body, grid=(vr // step,), in_specs=[spec(norm.shape, True)...]
    convert_element_type x4 -> x0, other arithmetic: 5.01 us -> none  [apply_update(): return (updated, momentum, variance, average, updated.astype(BF))]
    add x6 -> x0, other arithmetic: 4.22 us -> none  [the longest x5 3.26 us: apply_update(): average = 0.999 * shadow + 0.001 * updated]
where the time goes in v2:
time: 293 us
  Pallas kernels  292 us (100%)
    pallas_call x1, Pallas kernels, run_layers(): pl.pallas_call(body, out_shape=[jax.ShapeDtypeStruct(shape, F32) for _, s...  282 us
    pallas_call x1, Pallas kernels, run_update(): pl.pallas_call(body, grid=(vr // step,), in_specs=[spec(norm.shape, True)...  9.52 us

profile of v2, /device:TPU:0, one launch (start us, length us, event | category | flops | bytes accessed | tf_op | source)
XLA Modules:
  0.0 292.9 jit_solution(13760710440301827474)
XLA Ops:
  0.7 282.5 %shard_map.456 = (f32[512,1024]{1,0:T(8,128)}, f32[512,1024]{1,0:T(8,128)}, f32[3,128,256]{2,1,0:T(8,128)}, f32[128,256]{1,0:T(8,128)}, f32[128,1024]{1,0:T(8,12...) custom-call(bf16[512,1024]{1,0:T(8,128)(2,1)} %refs_0_.1, s32[1,96]{1,0:T(1,128)} %refs_1_.1, ...), custom_call_target="tpu_custom_call" | custom-call | flops 20000000000 | bytes 20000000 | tf_op jit(solution)/shard_map/pallas_call | solution.py:1123
  283.2 9.5 %shard_map.457 = (f32[3,128,256]{2,1,0:T(8,128)}, f32[3,128,256]{2,1,0:T(8,128)}, f32[3,128,256]{2,1,0:T(8,128)}, f32[3,128,256]{2,1,0:T(8,128)}, bf16[3,128,256...) custom-call(f32[8,128]{1,0:T(8,128)} %get-tuple-element.64.refs_0_, ...), custom_call_target="tpu_custom_call" | custom-call | flops 7872000 | bytes 15744000 | tf_op jit(solution)/shard_map/pallas_call | solution.py:1195

commit v3 on v2

--- a/solution.py
+++ b/solution.py
@@ -66,6 +66,7 @@
 def layer_kernel(names, sizes, *refs):
     r = SimpleNamespace(**dict(zip(names, refs, strict=True)))
     n, d_model, rows, hw, uw, vr = sizes
+    r.doz, r.dozt = r.qz.at[1], r.qzt.at[1]
     half = rows // 2
     ch = half // CHUNKS
     lines = n // 2
@@ -122,6 +123,13 @@
     each(0, lines, lambda s: greet(zy_peer(s)))
     pl.semaphore_wait(barrier, len(model_peers) + n - 1)
 
+    relay = lines == 4
+    crossing = (VEC, REJ)
+    last_line = lines - 1
+    inner = jnp.logical_and(z > 0, z < last_line)
+    far_end = (jnp.where(z == 1, 0, last_line) * 2 + y, m)
+    near_mid = (jnp.where(z == 0, 1, last_line - 1) * 2 + y, m)
+
     def gather_z(region, step):
         piece = block(weights[region], region, d)
         return remote(
@@ -134,33 +142,64 @@
             piece, piece, r.agzs.at[region, step], r.agzr.at[region, step], z_peer(step)
         )
 
+    def gather_relay(region):
+        piece = block(weights[region], region, z_from(2))
+        arrives_as = jnp.where(z == 1, 1, last_line)
+        return remote(
+            piece, piece, r.agzs.at[region, lines], r.agzr.at[region, arrives_as], far_end
+        )
+
     def gather_y(region, step):
         piece = block(weights[region], region, z_from(step))
         return remote(piece, piece, r.agys.at[region, step], r.agyr.at[region, step], y_peer)
 
+    def gather_cross(region, step):
+        piece = block(weights[region], region, d + 1 - 2 * y)
+        return remote(
+            piece, piece, r.agys.at[region, step], r.agyr.at[region, step], z_peer(step)
+        )
+
     def gather_y_arrival(region, step):
         piece = block(weights[region], region, z_from(step) + 1 - 2 * y)
         return remote(piece, piece, r.agys.at[region, step], r.agyr.at[region, step], y_peer)
 
-    def gather_start(region):
-        each(1, lines, lambda s: gather_z(region, s).start())
+    def near(region, step, body):
+        if not relay or region in crossing or step == 2:
+            body()
+        else:
+            pl.when(z < last_line if step == 1 else z > 0)(body)
+
+    def gather_start_z(region):
+        order = (1, 3, 2) if relay else range(1, lines)
+        for step in order:
+            near(region, step, lambda: gather_z(region, step).start())
+
+    def gather_start_y(region):
         gather_y(region, 0).start()
 
-    def gather_pass(region, only=None):
-        def one(step):
-            gather_z_arrival(region, step).wait_recv()
-            gather_y(region, step).start()
-
-        if only is None:
-            each(1, lines, one)
+    def gather_pass(region, turn):
+        step = jnp.where(z == 0, lines - turn, turn) if relay else turn
+        gather_z_arrival(region, step).wait_recv()
+        if relay and turn == 2:
+            pl.when(inner)(lambda: gather_relay(region).start())
+        gather_y(region, step).start()
+
+    def gather_turn(region):
+        gather_y_arrival(region, 0).wait_recv()
+        each(1, lines, lambda s: gather_cross(region, s).start())
+
+    def gather_wait(region):
+        if region in crossing:
+            each(1, lines, lambda s: gather_z_arrival(region, s).wait_recv())
+            each(1, lines, lambda s: gather_y_arrival(region, s).wait_recv())
         else:
-            one(only)
-
-    def gather_wait(region):
-        each(0, lines, lambda s: gather_y_arrival(region, s).wait_recv())
+            each(0, lines, lambda s: gather_y_arrival(region, s).wait_recv())
 
     def gather_close(region):
-        each(1, lines, lambda s: gather_z(region, s).wait_send())
+        for step in range(1, lines):
+            near(region, step, lambda: gather_z(region, step).wait_send())
+        if relay and region not in crossing:
+            pl.when(inner)(lambda: gather_relay(region).wait_send())
         each(0, lines, lambda s: gather_y(region, s).wait_send())
 
     def scatter_y(region, step):
@@ -173,39 +212,96 @@
             y_peer,
         )
 
+    def scatter_cross(region, step):
+        owner = ((z + step) % lines) * 2 + 1 - y
+        return remote(
+            block(grads[region], region, owner),
+            from_y[region].at[step],
+            r.rsys.at[region, step],
+            r.rsyr.at[region, step],
+            z_peer(step),
+        )
+
     def scatter_z(region, step):
         owner = ((z + step) % lines) * 2 + y
         return remote(
             block(grads[region], region, owner),
-            from_z[region].at[step - 1],
+            from_z[region].at[step],
             r.rszs.at[region, step],
             r.rszr.at[region, step],
             z_peer(step),
         )
 
+    def scatter_far(region, step):
+        owner = ((z + step) % lines) * 2 + y
+        return remote(
+            block(grads[region], region, owner),
+            from_z[region].at[0],
+            r.rszs.at[region, step],
+            r.rszr.at[region, 0],
+            near_mid,
+        )
+
+    def scatter_order(turn):
+        if not relay:
+            return turn % lines
+        if turn == 1:
+            return jnp.where(z == 0, last_line, 1)
+        if turn == 2:
+            return jnp.where(z == 0, 1, last_line)
+        return 2 if turn == 3 else 0
+
     def scatter_start(region):
-        def one(step):
-            scatter_y(region, step).start()
-
-        each(1, lines, one)
-        one(0)
-
-    def scatter_pass(region, step):
+        if region in crossing:
+            each(1, lines, lambda s: scatter_z(region, s).start())
+            each(1, lines, lambda s: scatter_cross(region, s).start())
+        else:
+            each(1, lines + 1, lambda t: scatter_y(region, scatter_order(t)).start())
+
+    def scatter_pass(region, turn):
+        step = scatter_order(turn)
         scatter_y(region, step).wait_recv()
         piece = block(grads[region], region, ((z + step) % lines) * 2 + y)
-        piece[...] = (piece[...].astype(F32) + from_y[region][step].astype(F32)).astype(BF)
-        scatter_z(region, step).start()
+        total = piece[...].astype(F32) + from_y[region][step].astype(F32)
+        piece[...] = total.astype(BF)
+        if not relay:
+            scatter_z(region, step).start()
+        elif turn == 1:
+            pl.when(inner)(lambda: scatter_z(region, step).start())
+            pl.when(jnp.logical_not(inner))(lambda: scatter_far(region, step).start())
+        elif turn == 2:
+            scatter_z(region, step).start()
+        else:
+
+            @pl.when(inner)
+            def _():
+                scatter_far(region, 0).wait_recv()
+                piece[...] = (total + from_z[region][0].astype(F32)).astype(BF)
+
+            scatter_z(region, step).start()
+
+    def scatter_turn(region):
+        piece = block(grads[region], region, d + 1 - 2 * y)
+        total = piece[...].astype(F32)
+        for step in range(1, lines):
+            scatter_cross(region, step).wait_recv()
+            total = total + from_y[region][step].astype(F32)
+        piece[...] = total.astype(BF)
+        scatter_y(region, 0).start()
 
     def scatter_finish(region, out_ref):
+        def one(step):
+            scatter_z(region, step).wait_recv()
+            out_ref[...] += from_z[region][step].astype(F32)
+
         scatter_y(region, 0).wait_recv()
         piece = block(grads[region], region, d)
         out_ref[...] = piece[...].astype(F32) + from_y[region][0].astype(F32)
-
-        def one(step):
-            scatter_z(region, step).wait_recv()
-            out_ref[...] += from_z[region][step - 1].astype(F32)
-
-        each(1, lines, one)
+        for step in range(1, lines):
+            if not relay or region in crossing or step == 2:
+                one(step)
+            else:
+                pl.when(z > 0 if step == 1 else z < last_line)(lambda: one(step))
 
     def scatter_close(region):
         each(0, lines, lambda s: scatter_y(region, s).wait_send())
@@ -285,18 +381,23 @@
     swap.start()
     mine = aligned(d * vr, vr)
     r.wa[:, mine, :] = r.attend[...].astype(BF)
-    gather_start(ATT)
+    gather_start_y(ATT)
+    gather_start_z(ATT)
     r.wr[mine, :] = r.rejoin[...].astype(BF)
+    gather_start_y(REJ)
     swap.wait_recv()
     r.vb[2] = r.vb[0] + r.vb[1]
     swap_x = remote(r.vb.at[2], r.vb.at[3], r.vxs.at[1], r.vxr.at[1], x_peer)
     swap_x.start()
     r.we[mine, :] = r.expand[...].astype(BF)
+    gather_start_y(EXP)
     r.wn[mine, :] = r.narrow[...].astype(BF)
     swap_x.wait_recv()
     r.wv[mine, :] = r.vb[2] + r.vb[3]
-    gather_start(VEC)
-    gather_start(REJ)
+    gather_start_y(VEC)
+    gather_start_y(NAR)
+    gather_start_z(VEC)
+    gather_start_z(REJ)
 
     r.pb[...] = jnp.full(r.pb.shape, SEQ_LEN, jnp.int32)
     slots = r.pos.shape[1]
@@ -326,6 +427,9 @@
     r.mc[0:slots, :] = r.mcot[...].reshape(slots, d_model)
     r.vg[...] = jnp.zeros(r.vg.shape, F32)
 
+    if relay:
+        gather_pass(ATT, 1)
+
     def embed(i):
         where = aligned(i * SUB, SUB)
         hot = r.oht[where, :]
@@ -342,11 +446,11 @@
                 source[row0 + i * LANES : row0 + (i + 1) * LANES, :]
             )
 
-    transpose_into(r.xt, 0, r.xl, 0, rows)
-
-    gather_pass(ATT)
-    gather_start(EXP)
-    gather_pass(VEC)
+    gather_turn(REJ)
+    gather_turn(VEC)
+    for turn in range(2 if relay else 1, lines):
+        gather_pass(ATT, turn)
+    gather_start_z(EXP)
     gather_wait(ATT)
     gather_wait(VEC)
     for j in range(d_model // LANES):
@@ -380,8 +484,7 @@
         ref[:, aligned(oth0 + q * ch, ch)] = across[:, :ch]
         ref[:, aligned(own0 + q * ch, ch)] = across[:, ch:]
 
-    for ref in (r.qzt, r.dozt):
-        ref[...] = jnp.zeros(ref.shape, BF)
+    r.qzt[...] = jnp.zeros(r.qzt.shape, BF)
 
     def share_block(layer, head, lane0, width):
         if layer == 0:
@@ -540,16 +643,17 @@
             if layer > 0:
                 share_wait(2 * layer - 1, r.xl, q)
             project(layer, q)
-        if layer == 0:
-            gather_pass(REJ)
         for q in range(CHUNKS):
             attend_forward(layer, q)
             if layer == 0 and q == 0:
+                gather_pass(EXP, 1)
+                gather_start_z(NAR)
                 gather_wait(REJ)
             rejoin_sum(layer, q)
         if layer == 0:
-            gather_start(NAR)
-            gather_pass(EXP)
+            for turn in range(2, lines):
+                gather_pass(EXP, turn)
+            transpose_into(r.xt, 0, r.xl, 0, rows)
         else:
             transpose_into(r.xt, rows, r.xl, 0, rows)
         for q in range(CHUNKS):
@@ -562,19 +666,23 @@
             widen(layer, q)
             if layer > 0:
                 narrow_sum(layer, q)
+            elif q == 0:
+                gather_pass(NAR, 1)
         if layer == 0:
             transpose_into(r.nt, 0, r.normed, 0, rows)
             if by_columns:
-                for step in range(lines):
-                    if step < lines - 1:
-                        gather_pass(NAR, step + 1)
+                for turn in range(lines):
+                    if 0 < turn < lines - 1:
+                        gather_pass(NAR, turn + 1)
+                    step = jnp.where(z == 0, (lines - turn) % lines, turn) if relay else turn
                     gather_y_arrival(NAR, step).wait_recv()
                     column_sum(step)
                 for step in range(lines):
                     column_x(step).wait()
                     column_core(step).wait_send()
             else:
-                gather_pass(NAR)
+                for turn in range(2, lines):
+                    gather_pass(NAR, turn)
                 gather_wait(NAR)
                 for q in range(CHUNKS):
                     narrow_sum(layer, q)
@@ -781,13 +889,13 @@
         if q == CHUNKS - 1:
             if by_columns:
 
-                def first_rows(step):
+                def first_rows(turn):
+                    step = scatter_order(turn)
                     owner = ((z + step) % lines) * 2 + 1 - y
                     weight_grad_rows(r.gsn, r.l2t, r.act0, uw, owner * vr, vr)
                     scatter_y(NAR, step).start()
 
-                each(1, lines, first_rows)
-                first_rows(0)
+                each(1, lines + 1, first_rows)
             else:
                 weight_grad(r.gsn, r.l2t, r.act0, uw)
                 scatter_start(NAR)
@@ -895,10 +1003,12 @@
     in_here.start()
     in_there.start()
 
+    pump()
+    scatter_turn(REJ)
+    scatter_turn(VEC)
     pump(len(passes))
-    each(1, lines, lambda s: scatter_pass(REJ, s))
-    each(1, lines, lambda s: scatter_pass(VEC, s))
-    each(1, lines, lambda s: scatter_pass(ATT, s))
+    for turn in range(1, lines):
+        scatter_pass(ATT, turn)
 
     def squares(value):
         value = value * value
@@ -976,7 +1086,6 @@
     hw = rejoin.shape[1]
     uw = expand.shape[1]
     lines = n // 2
-    ways = max(lines - 1, 1)
     half = rows // 2
     ch = half // CHUNKS
     heads = hw // HEAD_DIM
@@ -1019,11 +1128,11 @@
         ("yr", (lines, vr, hw)),
         ("ye", (lines, vr, uw)),
         ("yn", (lines, vr, uw)),
-        ("zv", (ways, vr, LANES)),
-        ("za", (ways, 3, vr, hw)),
-        ("zr", (ways, vr, hw)),
-        ("ze", (ways, vr, uw)),
-        ("zn", (ways, vr, uw)),
+        ("zv", (lines, vr, LANES)),
+        ("za", (lines, 3, vr, hw)),
+        ("zr", (lines, vr, hw)),
+        ("ze", (lines, vr, uw)),
+        ("zn", (lines, vr, uw)),
         ("cs", (2, CHUNKS, ch, d_model)),
         ("cr", (2, CHUNKS, ch, d_model)),
         ("xs", (2, CHUNKS, ch, d_model)),
@@ -1053,8 +1162,6 @@
         ("vvt", (hw, rows)),
         ("ct", (2, hw, rows)),
         ("p0", (heads, rows, rows)),
-        ("doz", (heads, rows, LANES)),
-        ("dozt", (heads, LANES, rows)),
         ("dqt", (hw, rows)),
         ("slc", (SLOTS, uw)),
         ("low2c", (SLOTS, d_model)),
@@ -1081,7 +1188,7 @@
         ("nz", (n, 8, LANES)),
     ]
     sems = [
-        ("agzs", (5, lines)),
+        ("agzs", (5, lines + 1)),
         ("agzr", (5, lines)),
         ("agys", (5, lines)),
         ("agyr", (5, lines)),

time: 293 us -> 284 us (0.969)
  Pallas kernels: 292 us -> 283 us
    pallas_call x1, Pallas kernels: 282 us -> 273 us  [run_layers(): pl.pallas_call(body, out_shape=[jax.ShapeDtypeStruct(shape, F32) for _, s...]
where the time goes in v3:
time: 284 us
  Pallas kernels  283 us (100%)
    pallas_call x1, Pallas kernels, run_layers(): pl.pallas_call(body, out_shape=[jax.ShapeDtypeStruct(shape, F32) for _, s...  273 us
    pallas_call x1, Pallas kernels, run_update(): pl.pallas_call(body, grid=(vr // step,), in_specs=[spec(norm.shape, True)...  9.52 us

profile of v3, /device:TPU:0, one launch (start us, length us, event | category | flops | bytes accessed | tf_op | source)
XLA Modules:
  0.0 283.9 jit_solution(17501787423487950513)
XLA Ops:
  0.7 273.5 %shard_map.456 = (f32[512,1024]{1,0:T(8,128)}, f32[512,1024]{1,0:T(8,128)}, f32[3,128,256]{2,1,0:T(8,128)}, f32[128,256]{1,0:T(8,128)}, f32[128,1024]{1,0:T(8,12...) custom-call(bf16[512,1024]{1,0:T(8,128)(2,1)} %refs_0_.1, s32[1,96]{1,0:T(1,128)} %refs_1_.1, ...), custom_call_target="tpu_custom_call" | custom-call | flops 20000000000 | bytes 20000000 | tf_op jit(solution)/shard_map/pallas_call | solution.py:1230
  274.2 9.5 %shard_map.457 = (f32[3,128,256]{2,1,0:T(8,128)}, f32[3,128,256]{2,1,0:T(8,128)}, f32[3,128,256]{2,1,0:T(8,128)}, f32[3,128,256]{2,1,0:T(8,128)}, bf16[3,128,256...) custom-call(f32[8,128]{1,0:T(8,128)} %get-tuple-element.64.refs_0_, ...), custom_call_target="tpu_custom_call" | custom-call | flops 7872000 | bytes 15744000 | tf_op jit(solution)/shard_map/pallas_call | solution.py:1302

commit v4 on v3

--- a/solution.py
+++ b/solution.py
@@ -124,7 +124,6 @@
     pl.semaphore_wait(barrier, len(model_peers) + n - 1)
 
     relay = lines == 4
-    crossing = (VEC, REJ)
     last_line = lines - 1
     inner = jnp.logical_and(z > 0, z < last_line)
     far_end = (jnp.where(z == 1, 0, last_line) * 2 + y, m)
@@ -142,64 +141,68 @@
             piece, piece, r.agzs.at[region, step], r.agzr.at[region, step], z_peer(step)
         )
 
-    def gather_relay(region):
-        piece = block(weights[region], region, z_from(2))
-        arrives_as = jnp.where(z == 1, 1, last_line)
+    def gather_onward(region, turn):
+        piece = block(weights[region], region, z_from(gather_order(turn)))
+        if turn == 3:
+            target = far_end
+            arrives_as = jnp.where(z == 1, 1, last_line)
+        else:
+            target = ((z + 3 - 2 * turn) * 2 + y, m)
+            arrives_as = 2
         return remote(
-            piece, piece, r.agzs.at[region, lines], r.agzr.at[region, arrives_as], far_end
+            piece,
+            piece,
+            r.agzs.at[region, last_line + turn],
+            r.agzr.at[region, arrives_as],
+            target,
         )
 
     def gather_y(region, step):
         piece = block(weights[region], region, z_from(step))
         return remote(piece, piece, r.agys.at[region, step], r.agyr.at[region, step], y_peer)
 
-    def gather_cross(region, step):
-        piece = block(weights[region], region, d + 1 - 2 * y)
-        return remote(
-            piece, piece, r.agys.at[region, step], r.agyr.at[region, step], z_peer(step)
-        )
-
     def gather_y_arrival(region, step):
         piece = block(weights[region], region, z_from(step) + 1 - 2 * y)
         return remote(piece, piece, r.agys.at[region, step], r.agyr.at[region, step], y_peer)
 
-    def near(region, step, body):
-        if not relay or region in crossing or step == 2:
+    def near(step, body):
+        if not relay:
             body()
-        else:
+        elif step != 2:
             pl.when(z < last_line if step == 1 else z > 0)(body)
 
     def gather_start_z(region):
-        order = (1, 3, 2) if relay else range(1, lines)
-        for step in order:
-            near(region, step, lambda: gather_z(region, step).start())
+        for step in range(1, lines):
+            near(step, lambda: gather_z(region, step).start())
 
     def gather_start_y(region):
         gather_y(region, 0).start()
 
+    def gather_order(turn):
+        if not relay or turn == 0:
+            return turn
+        if turn == 1:
+            return jnp.where(z == 0, last_line, 1)
+        if turn == 2:
+            return jnp.where(inner, last_line, 2)
+        return jnp.where(inner, 2, jnp.where(z == 0, 1, last_line))
+
     def gather_pass(region, turn):
-        step = jnp.where(z == 0, lines - turn, turn) if relay else turn
+        step = gather_order(turn)
         gather_z_arrival(region, step).wait_recv()
-        if relay and turn == 2:
-            pl.when(inner)(lambda: gather_relay(region).start())
+        if relay:
+            pl.when(inner)(lambda: gather_onward(region, turn).start())
         gather_y(region, step).start()
 
-    def gather_turn(region):
-        gather_y_arrival(region, 0).wait_recv()
-        each(1, lines, lambda s: gather_cross(region, s).start())
-
     def gather_wait(region):
-        if region in crossing:
-            each(1, lines, lambda s: gather_z_arrival(region, s).wait_recv())
-            each(1, lines, lambda s: gather_y_arrival(region, s).wait_recv())
-        else:
-            each(0, lines, lambda s: gather_y_arrival(region, s).wait_recv())
+        each(0, lines, lambda s: gather_y_arrival(region, s).wait_recv())
 
     def gather_close(region):
         for step in range(1, lines):
-            near(region, step, lambda: gather_z(region, step).wait_send())
-        if relay and region not in crossing:
-            pl.when(inner)(lambda: gather_relay(region).wait_send())
+            near(step, lambda: gather_z(region, step).wait_send())
+        if relay:
+            for turn in range(1, lines):
+                pl.when(inner)(lambda: gather_onward(region, turn).wait_send())
         each(0, lines, lambda s: gather_y(region, s).wait_send())
 
     def scatter_y(region, step):
@@ -212,16 +215,6 @@
             y_peer,
         )
 
-    def scatter_cross(region, step):
-        owner = ((z + step) % lines) * 2 + 1 - y
-        return remote(
-            block(grads[region], region, owner),
-            from_y[region].at[step],
-            r.rsys.at[region, step],
-            r.rsyr.at[region, step],
-            z_peer(step),
-        )
-
     def scatter_z(region, step):
         owner = ((z + step) % lines) * 2 + y
         return remote(
@@ -252,15 +245,31 @@
         return 2 if turn == 3 else 0
 
     def scatter_start(region):
-        if region in crossing:
-            each(1, lines, lambda s: scatter_z(region, s).start())
-            each(1, lines, lambda s: scatter_cross(region, s).start())
-        else:
-            each(1, lines + 1, lambda t: scatter_y(region, scatter_order(t)).start())
-
-    def scatter_pass(region, turn):
+        ready.append(region)
+        scatter_next()
+
+    ready = []
+    order = (NAR, EXP, REJ, VEC, ATT)
+    queue = [(region, turn) for region in order for turn in range(1, lines + 1)]
+    under_way = []
+    weight_of = {NAR: 4, EXP: 4, ATT: 3, REJ: 1, VEC: 1}
+
+    def scatter_next():
+        while queue and queue[0][0] in ready:
+            if sum(weight_of[region] for region, _ in under_way) > 4:
+                break
+            region, turn = queue.pop(0)
+            scatter_y(region, scatter_order(turn)).start()
+            under_way.append((region, turn))
+
+    def scatter_pass():
+        region, turn = under_way[0]
         step = scatter_order(turn)
         scatter_y(region, step).wait_recv()
+        under_way.pop(0)
+        scatter_next()
+        if turn == lines:
+            return
         piece = block(grads[region], region, ((z + step) % lines) * 2 + y)
         total = piece[...].astype(F32) + from_y[region][step].astype(F32)
         piece[...] = total.astype(BF)
@@ -280,25 +289,15 @@
 
             scatter_z(region, step).start()
 
-    def scatter_turn(region):
-        piece = block(grads[region], region, d + 1 - 2 * y)
-        total = piece[...].astype(F32)
-        for step in range(1, lines):
-            scatter_cross(region, step).wait_recv()
-            total = total + from_y[region][step].astype(F32)
-        piece[...] = total.astype(BF)
-        scatter_y(region, 0).start()
-
     def scatter_finish(region, out_ref):
         def one(step):
             scatter_z(region, step).wait_recv()
             out_ref[...] += from_z[region][step].astype(F32)
 
-        scatter_y(region, 0).wait_recv()
         piece = block(grads[region], region, d)
         out_ref[...] = piece[...].astype(F32) + from_y[region][0].astype(F32)
         for step in range(1, lines):
-            if not relay or region in crossing or step == 2:
+            if not relay or step == 2:
                 one(step)
             else:
                 pl.when(z > 0 if step == 1 else z < last_line)(lambda: one(step))
@@ -390,14 +389,10 @@
     swap_x = remote(r.vb.at[2], r.vb.at[3], r.vxs.at[1], r.vxr.at[1], x_peer)
     swap_x.start()
     r.we[mine, :] = r.expand[...].astype(BF)
-    gather_start_y(EXP)
     r.wn[mine, :] = r.narrow[...].astype(BF)
     swap_x.wait_recv()
     r.wv[mine, :] = r.vb[2] + r.vb[3]
     gather_start_y(VEC)
-    gather_start_y(NAR)
-    gather_start_z(VEC)
-    gather_start_z(REJ)
 
     r.pb[...] = jnp.full(r.pb.shape, SEQ_LEN, jnp.int32)
     slots = r.pos.shape[1]
@@ -427,8 +422,8 @@
     r.mc[0:slots, :] = r.mcot[...].reshape(slots, d_model)
     r.vg[...] = jnp.zeros(r.vg.shape, F32)
 
-    if relay:
-        gather_pass(ATT, 1)
+    gather_pass(ATT, 1)
+    gather_start_y(EXP)
 
     def embed(i):
         where = aligned(i * SUB, SUB)
@@ -446,13 +441,21 @@
                 source[row0 + i * LANES : row0 + (i + 1) * LANES, :]
             )
 
-    gather_turn(REJ)
-    gather_turn(VEC)
-    for turn in range(2 if relay else 1, lines):
+    for turn in range(2, lines - 1):
         gather_pass(ATT, turn)
+    gather_start_z(VEC)
+    gather_start_z(REJ)
+    gather_pass(ATT, lines - 1)
     gather_start_z(EXP)
+    for turn in range(1, lines):
+        gather_pass(VEC, turn)
+    for turn in range(1, lines):
+        gather_pass(REJ, turn)
+    gather_wait(VEC)
+    gather_pass(EXP, 1)
     gather_wait(ATT)
-    gather_wait(VEC)
+    gather_start_y(NAR)
+    gather_pass(EXP, 2)
     for j in range(d_model // LANES):
         r.vt[:, j * LANES : (j + 1) * LANES] = jnp.transpose(
             r.wv[j * LANES : (j + 1) * LANES, :].astype(F32), (1, 0)
@@ -565,24 +568,34 @@
     def unit_act(layer):
         return r.act0 if layer == 0 else r.gsn
 
-    def unit_slope(layer):
-        return (r.slope0, 0) if layer == 0 else (r.gsn, rows)
+    def gelu(v):
+        square = v * v
+        t = jnp.tanh(GELU_A * v * (1.0 + GELU_B * square))
+        return 0.5 * (1.0 + t), t, square
+
+    def gelu_slope(v, gate, t, square):
+        return gate + (0.5 * GELU_A) * v * (1.0 - t * t) * (1.0 + (3.0 * GELU_B) * square)
 
     def widen(layer, q):
         act = unit_act(layer)
-        slope, slope0 = unit_slope(layer)
 
         def one(j):
             cols = aligned(j * TILE, TILE)
             v = nn(both(r.normed, q), r.we[:, cols]) + r.vt[pl.ds(8 + m, 1), cols]
-            square = v * v
-            t = jnp.tanh(GELU_A * v * (1.0 + GELU_B * square))
-            gate = 0.5 * (1.0 + t)
+            gate, t, square = gelu(v)
             put_both(act, q, cols, (v * gate).astype(BF))
-            bend = gate + (0.5 * GELU_A) * v * (1.0 - t * t) * (1.0 + (3.0 * GELU_B) * square)
-            bend = bend.astype(BF)
-            slope[aligned(slope0 + oth0 + q * ch, ch), cols] = bend[:ch]
-            slope[aligned(slope0 + own0 + q * ch, ch), cols] = bend[ch:]
+            if layer == 0:
+                put_both(r.slope0, q, cols, gelu_slope(v, gate, t, square).astype(BF))
+
+        loop(uw // TILE, one)
+
+    def widen_slots():
+        def one(j):
+            cols = aligned(j * TILE, TILE)
+            v = nn(r.low2c[...], r.we[:, cols]) + r.vt[pl.ds(8 + m, 1), cols]
+            gate, t, square = gelu(v)
+            r.act0[rows : rows + SLOTS, cols] = (v * gate).astype(BF)
+            r.slc[:, cols] = gelu_slope(v, gate, t, square).astype(BF)
 
         loop(uw // TILE, one)
 
@@ -645,14 +658,17 @@
             project(layer, q)
         for q in range(CHUNKS):
             attend_forward(layer, q)
-            if layer == 0 and q == 0:
-                gather_pass(EXP, 1)
+            if layer > 0:
+                rejoin_sum(layer, q)
+            elif q == 0:
+                for turn in range(3, lines):
+                    gather_pass(EXP, turn)
                 gather_start_z(NAR)
-                gather_wait(REJ)
-            rejoin_sum(layer, q)
         if layer == 0:
-            for turn in range(2, lines):
-                gather_pass(EXP, turn)
+            gather_wait(REJ)
+            for q in range(CHUNKS):
+                rejoin_sum(layer, q)
+            gather_pass(NAR, 1)
             transpose_into(r.xt, 0, r.xl, 0, rows)
         else:
             transpose_into(r.xt, rows, r.xl, 0, rows)
@@ -660,53 +676,41 @@
             sum_end(2 * layer, q, ch)
             first_norm(layer, q)
             share(2 * layer, r.normed, q).start()
-            if layer == 0 and q == 0:
-                gather_wait(EXP)
+            if layer == 0:
+                gather_pass(NAR, q + 2)
+                if q == 0:
+                    gather_wait(EXP)
             share_wait(2 * layer, r.normed, q)
             widen(layer, q)
             if layer > 0:
                 narrow_sum(layer, q)
-            elif q == 0:
-                gather_pass(NAR, 1)
         if layer == 0:
-            transpose_into(r.nt, 0, r.normed, 0, rows)
+            for turn in range(CHUNKS + 2, lines):
+                gather_pass(NAR, turn)
             if by_columns:
                 for turn in range(lines):
-                    if 0 < turn < lines - 1:
-                        gather_pass(NAR, turn + 1)
-                    step = jnp.where(z == 0, (lines - turn) % lines, turn) if relay else turn
+                    step = gather_order(turn)
                     gather_y_arrival(NAR, step).wait_recv()
                     column_sum(step)
+                transpose_into(r.nt, 0, r.normed, 0, rows)
                 for step in range(lines):
                     column_x(step).wait()
                     column_core(step).wait_send()
             else:
-                for turn in range(2, lines):
-                    gather_pass(NAR, turn)
+                transpose_into(r.nt, 0, r.normed, 0, rows)
                 gather_wait(NAR)
                 for q in range(CHUNKS):
                     narrow_sum(layer, q)
         else:
-            pick(r.act0, rows, r.gsn, 0, uw)
-            pick(r.slc, 0, r.gsn, rows, uw)
-            for head in range(heads):
-                r.qc[head] = nn(hot, r.qz[1, head]).astype(BF)
-                source = r.gse[
-                    (head // 2) * rows : (head // 2 + 1) * rows,
-                    (head % 2) * rows : (head % 2 + 1) * rows,
-                ]
-                r.pc[head] = nn(source, r.oht[...]).astype(BF)
+            pick(r.low2c, 0, r.normed, 0, d_model)
+            widen_slots()
+            transpose_into(r.nt, rows, r.low2c, 0, SLOTS)
         for q in range(CHUNKS):
             if not (layer == 0 and by_columns):
                 sum_end(2 * layer + 1, q, ch)
             second_norm(layer, q)
             if layer < DEPTH - 1:
                 share(2 * layer + 1, r.xl, q).start()
-            elif q == 0:
-                pick(r.low2c, 0, r.normed, 0, d_model)
-                transpose_into(r.nt, rows, r.low2c, 0, SLOTS)
-                pick(r.ctx, rows, r.ctx1, 0, hw)
-                r.cct[...] = nn(r.ct[1], r.oht[...]).astype(BF)
 
     own_rows = aligned(own0, half)
     out_here = pltpu.make_async_copy(r.st, r.act.at[own_rows], r.osem.at[0])
@@ -795,6 +799,14 @@
 
     sum_begin(4, 0, slot_tile, slot_half)
     transpose_into(r.l2t, rows, r.low2c, 0, SLOTS)
+    for head in range(heads):
+        r.qc[head] = nn(hot, r.qz[1, head]).astype(BF)
+        source = r.gse[
+            (head // 2) * rows : (head // 2 + 1) * rows,
+            (head % 2) * rows : (head % 2 + 1) * rows,
+        ]
+        r.pc[head] = nn(source, r.oht[...]).astype(BF)
+    r.cct[...] = nn(r.ct[1], r.oht[...]).astype(BF)
     sum_end(4, 0, slot_half)
     mine_slots = r.slt.at[aligned(slot_own, slot_half)]
     mine_slots[...] = sum_rows(4, 0, slice(0, slot_half)).astype(BF)
@@ -812,7 +824,6 @@
     for q in range(CHUNKS):
         share_wait(5, r.xl, q)
     pick(r.low2c, 0, r.xl, 0, d_model)
-    transpose_into(r.l1t, rows, r.low2c, 0, SLOTS)
     low_ctx = nn(r.low2c[...], r.wr[...]).astype(BF)
     across = low_transpose(low_ctx)
     dq_across = []
@@ -858,6 +869,7 @@
 
     for q in range(CHUNKS):
         layer_rows(5, q, rows)
+    transpose_into(r.l1t, rows, r.low2c, 0, SLOTS)
 
     def weight_grad_rows(target, across, latter, width, row0, count):
         at = aligned(row0, count)
@@ -878,38 +890,41 @@
         for row0 in (oth0 + q * ch, own0 + q * ch):
             target[:, aligned(row0, ch)] = low_transpose(source[aligned(row0, ch), :])
 
-    for q in range(CHUNKS):
-        sum_end(5, q, ch)
-        second_pull(
-            0, q, lambda i, at: r.gb[at, :] + sum_rows(5, q, aligned(i * SUB, SUB))
-        )
-        share(6, r.low2, q).start()
-        share_wait(6, r.low2, q)
-        transpose_both(r.l2t, r.low2, q)
-        if q == CHUNKS - 1:
-            if by_columns:
-
-                def first_rows(turn):
-                    step = scatter_order(turn)
-                    owner = ((z + step) % lines) * 2 + 1 - y
-                    weight_grad_rows(r.gsn, r.l2t, r.act0, uw, owner * vr, vr)
-                    scatter_y(NAR, step).start()
-
-                each(1, lines + 1, first_rows)
-            else:
-                weight_grad(r.gsn, r.l2t, r.act0, uw)
-                scatter_start(NAR)
-
-        def units(j, q=q):
+    def units_back(q):
+        def one(j):
             cols = aligned(j * TILE, TILE)
             slope = both(r.slope0, q, cols).astype(F32)
             back = (nn(both(r.low2, q), r.wn[:, cols]) * slope).astype(BF)
             put_both(r.be, q, cols, back)
             r.vg[pl.ds(8 + m, 1), cols] += jnp.sum(back.astype(F32), axis=0, keepdims=True)
 
-        loop(uw // TILE, units)
+        loop(uw // TILE, one)
+
+    for q in range(CHUNKS):
+        sum_end(5, q, ch)
+        second_pull(
+            0, q, lambda i, at: r.gb[at, :] + sum_rows(5, q, aligned(i * SUB, SUB))
+        )
+        share(6, r.low2, q).start()
+        share_wait(6, r.low2, q)
+        transpose_both(r.l2t, r.low2, q)
+        if q == 0:
+            units_back(q)
+    if by_columns:
+        for turn in range(1, lines + 1):
+            owner = ((z + scatter_order(turn)) % lines) * 2 + 1 - y
+            weight_grad_rows(r.gsn, r.l2t, r.act0, uw, owner * vr, vr)
+            if turn <= 2:
+                scatter_y(NAR, scatter_order(turn)).start()
+                under_way.append(queue.pop(0))
+        ready.append(NAR)
+    else:
+        weight_grad(r.gsn, r.l2t, r.act0, uw)
+        scatter_start(NAR)
+    for q in range(CHUNKS):
+        if q > 0:
+            units_back(q)
         sum_begin(6, q, lambda cols, q=q: nt(both(r.be, q), r.we[cols, :]), ch)
-
     if by_columns:
         each(
             0,
@@ -918,23 +933,17 @@
                 r.gsn, r.l2t, r.act0, uw, (((z + s) % lines) * 2 + y) * vr, vr
             ),
         )
+    pick(r.ctx, rows, r.ctx1, 0, hw)
     weight_grad(r.gse, r.nt, r.be, uw)
     scatter_start(EXP)
-    passes = [lambda s=s: scatter_pass(NAR, s) for s in range(1, lines)]
-    passes += [lambda s=s: scatter_pass(EXP, s) for s in range(1, lines)]
-
-    def pump(count=1):
-        for _ in range(min(count, len(passes))):
-            passes.pop(0)()
-
-    pump()
+    scatter_pass()
     for q in range(CHUNKS):
         sum_end(6, q, ch)
         first_pull(
             0, q, lambda i, at: r.gb[at, :] + sum_rows(6, q, aligned(i * SUB, SUB))
         )
         share(7, r.xl, q).start()
-    pump()
+    scatter_pass()
     for q in range(CHUNKS):
         share_wait(7, r.xl, q)
         back = nn(both(r.xl, q), r.wr[...]).astype(BF)
@@ -963,13 +972,17 @@
         r.dp[1, 0:rows, lanes] = dk.astype(BF)
         r.dp[2, 0:rows, lanes] = dv.astype(BF)
 
-    loop(heads // 2, head_pair)
+    for pair in range(heads // 2):
+        head_pair(pair)
+        if under_way[0][0] != REJ:
+            scatter_pass()
     for i in range(rows // LANES):
         some = slice(i * LANES, (i + 1) * LANES)
         r.dp[0, some, :] = low_transpose(r.dqt[:, some])
     for q in range(CHUNKS):
         layer_rows(7, q, 0)
-    pump()
+    if under_way[0][0] != REJ:
+        scatter_pass()
     bias_sums(0)
     transpose_into(r.l1t, 0, r.xl, 0, rows)
     weight_grad(r.gsr, r.l1t, r.ctx, hw)
@@ -985,7 +998,7 @@
     for kind in range(3):
         weight_grad(r.gsa.at[kind], r.xt, r.dp.at[kind], hw)
     scatter_start(ATT)
-    pump()
+    scatter_pass()
     out_here.wait()
     out_there.wait_send()
     for q in range(CHUNKS):
@@ -1003,13 +1016,7 @@
     in_here.start()
     in_there.start()
 
-    pump()
-    scatter_turn(REJ)
-    scatter_turn(VEC)
-    pump(len(passes))
-    for turn in range(1, lines):
-        scatter_pass(ATT, turn)
-
+    scatter_pass()
     def squares(value):
         value = value * value
         if value.ndim == 3:
@@ -1017,21 +1024,31 @@
         value = jnp.sum(value, axis=0, keepdims=True)
         return jnp.sum(value, axis=1, keepdims=True)
 
-    scatter_finish(NAR, r.gn)
-    scatter_finish(EXP, r.ge)
-    scatter_finish(REJ, r.gr)
-    total = squares(r.gn[...]) + squares(r.ge[...]) + squares(r.gr[...])
-    scatter_finish(VEC, r.vf.at[0])
     swap_v = remote(r.vf.at[0], r.vf.at[1], r.vxs.at[2], r.vxr.at[2], core_peer)
-    swap_v.start()
-    swap_v.wait_recv()
-    r.vf[2] = r.vf[0] + r.vf[1]
     swap_w = remote(r.vf.at[2], r.vf.at[3], r.vxs.at[3], r.vxr.at[3], x_peer)
-    swap_w.start()
-    swap_w.wait_recv()
-    r.vs[...] = jnp.transpose(r.vf[2] + r.vf[3], (1, 0))
-    r.gv[...] = r.vs[pl.ds(columns * m, columns), :]
-    total = total + squares(r.gv[...])
+    total = jnp.zeros((1, 1), F32)
+    while under_way:
+        turn = under_way[0][1] if under_way[0][0] == ATT else 0
+        if turn == 1:
+            scatter_finish(NAR, r.gn)
+            total = total + squares(r.gn[...])
+        elif turn == 2:
+            scatter_finish(VEC, r.vf.at[0])
+            swap_v.start()
+            scatter_finish(REJ, r.gr)
+            total = total + squares(r.gr[...])
+        elif turn == 3:
+            swap_v.wait_recv()
+            r.vf[2] = r.vf[0] + r.vf[1]
+            swap_w.start()
+            scatter_finish(EXP, r.ge)
+            total = total + squares(r.ge[...])
+        elif turn == 4:
+            swap_w.wait_recv()
+            r.vs[...] = jnp.transpose(r.vf[2] + r.vf[3], (1, 0))
+            r.gv[...] = r.vs[pl.ds(columns * m, columns), :]
+            total = total + squares(r.gv[...])
+        scatter_pass()
     scatter_finish(ATT, r.ga)
     total = total + squares(r.ga[...])
 
@@ -1188,7 +1205,7 @@
         ("nz", (n, 8, LANES)),
     ]
     sems = [
-        ("agzs", (5, lines + 1)),
+        ("agzs", (5, lines + 3)),
         ("agzr", (5, lines)),
         ("agys", (5, lines)),
         ("agyr", (5, lines)),

time: 284 us -> 265 us (0.933)
  Pallas kernels: 283 us -> 264 us
    pallas_call x1, Pallas kernels: 273 us -> 254 us  [run_layers(): pl.pallas_call(body, out_shape=[jax.ShapeDtypeStruct(shape, F32) for _, s...]
where the time goes in v4:
time: 265 us
  Pallas kernels  264 us (100%)
    pallas_call x1, Pallas kernels, run_layers(): pl.pallas_call(body, out_shape=[jax.ShapeDtypeStruct(shape, F32) for _, s...  254 us
    pallas_call x1, Pallas kernels, run_update(): pl.pallas_call(body, grid=(vr // step,), in_specs=[spec(norm.shape, True)...  9.52 us

profile of v4, /device:TPU:0, one launch (start us, length us, event | category | flops | bytes accessed | tf_op | source)
XLA Modules:
  0.0 264.7 jit_solution(16148402488648409509)
XLA Ops:
  0.7 254.4 %shard_map.456 = (f32[512,1024]{1,0:T(8,128)}, f32[512,1024]{1,0:T(8,128)}, f32[3,128,256]{2,1,0:T(8,128)}, f32[128,256]{1,0:T(8,128)}, f32[128,1024]{1,0:T(8,12...) custom-call(bf16[512,1024]{1,0:T(8,128)(2,1)} %refs_0_.1, s32[1,96]{1,0:T(1,128)} %refs_1_.1, ...), custom_call_target="tpu_custom_call" | custom-call | flops 20000000000 | bytes 20000000 | tf_op jit(solution)/shard_map/pallas_call | solution.py:1247
  255.0 9.5 %shard_map.457 = (f32[3,128,256]{2,1,0:T(8,128)}, f32[3,128,256]{2,1,0:T(8,128)}, f32[3,128,256]{2,1,0:T(8,128)}, f32[3,128,256]{2,1,0:T(8,128)}, bf16[3,128,256...) custom-call(f32[8,128]{1,0:T(8,128)} %get-tuple-element.64.refs_0_, ...), custom_call_target="tpu_custom_call" | custom-call | flops 7872000 | bytes 15744000 | tf_op jit(solution)/shard_map/pallas_call | solution.py:1319

commit v5 on v4

--- a/solution.py
+++ b/solution.py
@@ -99,6 +99,8 @@
         return ((z + lines - step) % lines) * 2 + y
 
     def block(ref, region, index):
+        if region == VEC:
+            return ref.at[index]
         where = aligned(index * vr, vr)
         return ref.at[:, where, :] if region == ATT else ref.at[where, :]
 
@@ -306,45 +308,46 @@
         each(0, lines, lambda s: scatter_y(region, s).wait_send())
         each(1, lines, lambda s: scatter_z(region, s).wait_send())
 
-    def core_copy(k, q, count):
-        b = k % 2
+    tiles = d_model // TILE
+
+    def core_copy(k, q, count, j):
+        where = (k % 2, q, slice(0, count), aligned(j * TILE, TILE))
         return remote(
-            r.cs.at[b, q, :count],
-            r.cr.at[b, q, :count],
-            r.arcs.at[k, q],
-            r.arcr.at[k, q],
-            core_peer,
-        )
-
-    def x_copy(k, q, count):
-        b = k % 2
+            r.cs.at[where], r.cr.at[where], r.arcs.at[k, q, j], r.arcr.at[k, q, j], core_peer
+        )
+
+    def x_copy(k, q, count, j):
+        where = (k % 2, q, slice(0, count), aligned(j * TILE, TILE))
         return remote(
-            r.xs.at[b, q, :count],
-            r.xr.at[b, q, :count],
-            r.arxs.at[k, q],
-            r.arxr.at[k, q],
-            x_peer,
+            r.xs.at[where], r.xr.at[where], r.arxs.at[k, q, j], r.arxr.at[k, q, j], x_peer
         )
 
     def sum_begin(k, q, tile_of, count):
         b = k % 2
+
+        def onward(j):
+            cols = aligned(j * TILE, TILE)
+            core_copy(k, q, count, j).wait_recv()
+            r.xs[b, q, :count, cols] = (
+                r.acc[:count, cols] + r.cr[b, q, :count, cols].astype(F32)
+            ).astype(BF)
+            x_copy(k, q, count, j).start()
 
         def one(j):
             cols = aligned(j * TILE, TILE)
             part = tile_of(cols)
             r.cs[b, q, :count, cols] = part[:count].astype(BF)
+            core_copy(k, q, count, j).start()
             r.acc[:count, cols] = part[count:]
-
-        loop(d_model // TILE, one)
-        copy = core_copy(k, q, count)
-        copy.start()
-        copy.wait_recv()
-        r.xs[b, q, :count] = (r.acc[:count] + r.cr[b, q, :count].astype(F32)).astype(BF)
-        x_copy(k, q, count).start()
+            pl.when(j > 0)(lambda: onward(j - 1))
+
+        loop(tiles, one)
+        onward(tiles - 1)
 
     def sum_end(k, q, count):
-        x_copy(k, q, count).wait()
-        core_copy(k, q, count).wait_send()
+        for j in range(tiles):
+            x_copy(k, q, count, j).wait()
+            core_copy(k, q, count, j).wait_send()
 
     def sum_rows(k, q, where):
         b = k % 2
@@ -375,7 +378,7 @@
     columns = r.vin.shape[0]
     r.vs[...] = jnp.zeros(r.vs.shape, F32)
     r.vs[pl.ds(columns * m, columns), :] = r.vin[...]
-    r.vb[0] = low_transpose(r.vs[...])
+    r.vb[0] = r.vs[...].astype(BF)
     swap = remote(r.vb.at[0], r.vb.at[1], r.vxs.at[0], r.vxr.at[0], core_peer)
     swap.start()
     mine = aligned(d * vr, vr)
@@ -391,7 +394,7 @@
     r.we[mine, :] = r.expand[...].astype(BF)
     r.wn[mine, :] = r.narrow[...].astype(BF)
     swap_x.wait_recv()
-    r.wv[mine, :] = r.vb[2] + r.vb[3]
+    r.wv[d] = r.vb[2] + r.vb[3]
     gather_start_y(VEC)
 
     r.pb[...] = jnp.full(r.pb.shape, SEQ_LEN, jnp.int32)
@@ -456,10 +459,8 @@
     gather_wait(ATT)
     gather_start_y(NAR)
     gather_pass(EXP, 2)
-    for j in range(d_model // LANES):
-        r.vt[:, j * LANES : (j + 1) * LANES] = jnp.transpose(
-            r.wv[j * LANES : (j + 1) * LANES, :].astype(F32), (1, 0)
-        )[0:16, :]
+    for j in range(n):
+        r.vt[:, j * vr : (j + 1) * vr] = r.wv[j].astype(F32)
 
     def head_bias(row):
         return r.vt[row : row + 1, aligned(m * hw, hw)]
@@ -989,11 +990,8 @@
     scatter_start(REJ)
     first_of_x = jnp.where(m < 2, 1.0, 0.0)
     r.vg[2:8, :] = r.vg[2:8, :] * first_of_x
-    for j in range(d_model // LANES):
-        tall = jnp.concatenate(
-            [r.vg[:, j * LANES : (j + 1) * LANES], jnp.zeros((LANES - 16, LANES), F32)], axis=0
-        )
-        r.gsv[j * LANES : (j + 1) * LANES, :] = jnp.transpose(tall, (1, 0)).astype(BF)
+    for j in range(n):
+        r.gsv[j] = r.vg[:, j * vr : (j + 1) * vr].astype(BF)
     scatter_start(VEC)
     for kind in range(3):
         weight_grad(r.gsa.at[kind], r.xt, r.dp.at[kind], hw)
@@ -1032,6 +1030,9 @@
         if turn == 1:
             scatter_finish(NAR, r.gn)
             total = total + squares(r.gn[...])
+            scatter_close(NAR)
+            for region in range(5):
+                gather_close(region)
         elif turn == 2:
             scatter_finish(VEC, r.vf.at[0])
             swap_v.start()
@@ -1043,9 +1044,11 @@
             swap_w.start()
             scatter_finish(EXP, r.ge)
             total = total + squares(r.ge[...])
+            scatter_close(EXP)
+            scatter_close(REJ)
         elif turn == 4:
             swap_w.wait_recv()
-            r.vs[...] = jnp.transpose(r.vf[2] + r.vf[3], (1, 0))
+            r.vs[...] = r.vf[2] + r.vf[3]
             r.gv[...] = r.vs[pl.ds(columns * m, columns), :]
             total = total + squares(r.gv[...])
         scatter_pass()
@@ -1086,9 +1089,8 @@
     swap_v.wait_send()
     swap_w.wait_send()
     slots_out.wait_send()
-    for region in range(5):
-        gather_close(region)
-        scatter_close(region)
+    scatter_close(VEC)
+    scatter_close(ATT)
     out_arrival.wait_recv()
     in_here.wait()
     in_there.wait_send()
@@ -1130,22 +1132,22 @@
         ("norm", (8, LANES), pltpu.VMEM),
     ]
     low = [
-        ("wv", (d_model, LANES)),
+        ("wv", (n, 16, vr)),
         ("wa", (3, d_model, hw)),
         ("wr", (d_model, hw)),
         ("we", (d_model, uw)),
         ("wn", (d_model, uw)),
-        ("gsv", (d_model, LANES)),
+        ("gsv", (n, 16, vr)),
         ("gsa", (3, d_model, hw)),
         ("gsr", (d_model, hw)),
         ("gse", (d_model, uw)),
         ("gsn", (d_model, uw)),
-        ("yv", (lines, vr, LANES)),
+        ("yv", (lines, 16, vr)),
         ("ya", (lines, 3, vr, hw)),
         ("yr", (lines, vr, hw)),
         ("ye", (lines, vr, uw)),
         ("yn", (lines, vr, uw)),
-        ("zv", (lines, vr, LANES)),
+        ("zv", (lines, 16, vr)),
         ("za", (lines, 3, vr, hw)),
         ("zr", (lines, vr, hw)),
         ("ze", (lines, vr, uw)),
@@ -1154,7 +1156,7 @@
         ("cr", (2, CHUNKS, ch, d_model)),
         ("xs", (2, CHUNKS, ch, d_model)),
         ("xr", (2, CHUNKS, ch, d_model)),
-        ("vb", (4, vr, LANES)),
+        ("vb", (4, 16, vr)),
         ("oh", (SLOTS, rows)),
         ("oht", (rows, SLOTS)),
         ("mc", (SLOTS, d_model)),
@@ -1199,8 +1201,8 @@
         ("rs2", (2, half, 1)),
         ("acc", (ch, d_model)),
         ("part", (SLOTS, TILE)),
-        ("vf", (4, vr, LANES)),
-        ("vs", (LANES, vr)),
+        ("vf", (4, 16, vr)),
+        ("vs", (16, vr)),
         ("nm", (4, 8, LANES)),
         ("nz", (n, 8, LANES)),
     ]
@@ -1213,10 +1215,10 @@
         ("rsyr", (5, lines)),
         ("rszs", (5, lines)),
         ("rszr", (5, lines)),
-        ("arcs", (8, CHUNKS)),
-        ("arcr", (8, CHUNKS)),
-        ("arxs", (8, CHUNKS)),
-        ("arxr", (8, CHUNKS)),
+        ("arcs", (8, CHUNKS, d_model // TILE)),
+        ("arcr", (8, CHUNKS, d_model // TILE)),
+        ("arxs", (8, CHUNKS, d_model // TILE)),
+        ("arxr", (8, CHUNKS, d_model // TILE)),
         ("shs", (8, CHUNKS)),
         ("shr", (8, CHUNKS)),
         ("vxs", (4,)),
@@ -1298,7 +1300,7 @@
 
 def run_update(groups, rates, norm, clip_limit, act, ing):
     vr = groups[1][0].shape[0]
-    step = min(vr, 32)
+    step = min(vr, 64)
 
     def spec(shape, whole):
         if whole:

time: 265 us -> 258 us (0.974)
  Pallas kernels: 264 us -> 257 us
    pallas_call x1, Pallas kernels: 254 us -> 249 us  [run_layers(): pl.pallas_call(body, out_shape=[jax.ShapeDtypeStruct(shape, F32) for _, s...]
where the time goes in v5:
time: 258 us
  Pallas kernels  257 us (100%)
    pallas_call x1, Pallas kernels, run_layers(): pl.pallas_call(body, out_shape=[jax.ShapeDtypeStruct(shape, F32) for _, s...  249 us
    pallas_call x1, Pallas kernels, run_update(): pl.pallas_call(body, grid=(vr // step,), in_specs=[spec(norm.shape, True)...  8.45 us

profile of v5, /device:TPU:0, one launch (start us, length us, event | category | flops | bytes accessed | tf_op | source)
XLA Modules:
  0.0 258.0 jit_solution(7824530529406630310)
XLA Ops:
  0.7 248.7 %shard_map.456 = (f32[512,1024]{1,0:T(8,128)}, f32[512,1024]{1,0:T(8,128)}, f32[3,128,256]{2,1,0:T(8,128)}, f32[128,256]{1,0:T(8,128)}, f32[128,1024]{1,0:T(8,12...) custom-call(bf16[512,1024]{1,0:T(8,128)(2,1)} %refs_0_.1, s32[1,96]{1,0:T(1,128)} %refs_1_.1, ...), custom_call_target="tpu_custom_call" | custom-call | flops 20000000000 | bytes 20000000 | tf_op jit(solution)/shard_map/pallas_call | solution.py:1249
  249.4 8.5 %shard_map.457 = (f32[3,128,256]{2,1,0:T(8,128)}, f32[3,128,256]{2,1,0:T(8,128)}, f32[3,128,256]{2,1,0:T(8,128)}, f32[3,128,256]{2,1,0:T(8,128)}, bf16[3,128,256...) custom-call(f32[8,128]{1,0:T(8,128)} %get-tuple-element.64.refs_0_, ...), custom_call_target="tpu_custom_call" | custom-call | flops 7872000 | bytes 15744000 | tf_op jit(solution)/shard_map/pallas_call | solution.py:1321

commit v6 on v5

--- a/solution.py
+++ b/solution.py
@@ -123,7 +123,6 @@
         greet(peer)
     each(1, lines, lambda s: greet(z_peer(s)))
     each(0, lines, lambda s: greet(zy_peer(s)))
-    pl.semaphore_wait(barrier, len(model_peers) + n - 1)
 
     relay = lines == 4
     last_line = lines - 1
@@ -246,15 +245,38 @@
             return jnp.where(z == 0, 1, last_line)
         return 2 if turn == 3 else 0
 
+    def scatter_cross(step):
+        owner = ((z + step) % lines) * 2 + 1 - y
+        return remote(
+            block(grads[REJ], REJ, owner),
+            from_y[REJ].at[step],
+            r.rsys.at[REJ, step],
+            r.rsyr.at[REJ, step],
+            z_peer(step),
+        )
+
+    def scatter_turn():
+        piece = block(grads[REJ], REJ, d + 1 - 2 * y)
+        total = piece[...].astype(F32)
+        for step in range(1, lines):
+            scatter_cross(step).wait_recv()
+            total = total + from_y[REJ][step].astype(F32)
+        piece[...] = total.astype(BF)
+        scatter_y(REJ, 0).start()
+
     def scatter_start(region):
+        if region == REJ:
+            each(1, lines, lambda s: scatter_z(REJ, s).start())
+            each(1, lines, lambda s: scatter_cross(s).start())
+            return
         ready.append(region)
         scatter_next()
 
     ready = []
-    order = (NAR, EXP, REJ, VEC, ATT)
+    order = (NAR, EXP, VEC, ATT)
     queue = [(region, turn) for region in order for turn in range(1, lines + 1)]
     under_way = []
-    weight_of = {NAR: 4, EXP: 4, ATT: 3, REJ: 1, VEC: 1}
+    weight_of = {NAR: 4, EXP: 4, ATT: 3, VEC: 1}
 
     def scatter_next():
         while queue and queue[0][0] in ready:
@@ -296,10 +318,12 @@
             scatter_z(region, step).wait_recv()
             out_ref[...] += from_z[region][step].astype(F32)
 
+        if region == REJ:
+            scatter_y(region, 0).wait_recv()
         piece = block(grads[region], region, d)
         out_ref[...] = piece[...].astype(F32) + from_y[region][0].astype(F32)
         for step in range(1, lines):
-            if not relay or step == 2:
+            if not relay or region == REJ or step == 2:
                 one(step)
             else:
                 pl.when(z > 0 if step == 1 else z < last_line)(lambda: one(step))
@@ -379,13 +403,14 @@
     r.vs[...] = jnp.zeros(r.vs.shape, F32)
     r.vs[pl.ds(columns * m, columns), :] = r.vin[...]
     r.vb[0] = r.vs[...].astype(BF)
+    mine = aligned(d * vr, vr)
+    r.wa[:, mine, :] = r.attend[...].astype(BF)
+    r.wr[mine, :] = r.rejoin[...].astype(BF)
+    pl.semaphore_wait(barrier, len(model_peers) + n - 1)
     swap = remote(r.vb.at[0], r.vb.at[1], r.vxs.at[0], r.vxr.at[0], core_peer)
     swap.start()
-    mine = aligned(d * vr, vr)
-    r.wa[:, mine, :] = r.attend[...].astype(BF)
     gather_start_y(ATT)
     gather_start_z(ATT)
-    r.wr[mine, :] = r.rejoin[...].astype(BF)
     gather_start_y(REJ)
     swap.wait_recv()
     r.vb[2] = r.vb[0] + r.vb[1]
@@ -975,15 +1000,13 @@
 
     for pair in range(heads // 2):
         head_pair(pair)
-        if under_way[0][0] != REJ:
-            scatter_pass()
+        scatter_pass()
     for i in range(rows // LANES):
         some = slice(i * LANES, (i + 1) * LANES)
         r.dp[0, some, :] = low_transpose(r.dqt[:, some])
     for q in range(CHUNKS):
         layer_rows(7, q, 0)
-    if under_way[0][0] != REJ:
-        scatter_pass()
+    scatter_pass()
     bias_sums(0)
     transpose_into(r.l1t, 0, r.xl, 0, rows)
     weight_grad(r.gsr, r.l1t, r.ctx, hw)
@@ -1013,6 +1036,7 @@
     in_arrival = remote(r.st, r.ing.at[aligned(oth0, half)], r.osem.at[6], r.osem.at[7], core_peer)
     in_here.start()
     in_there.start()
+    scatter_turn()
 
     scatter_pass()
     def squares(value):

time: 258 us -> 257 us (level)
  no operation moved by 1% of the time
where the time goes in v6:
time: 257 us; the launch traced here: 256 us
  Pallas kernels  256 us (100%)
    pallas_call x1, Pallas kernels, run_layers(): pl.pallas_call(body, out_shape=[jax.ShapeDtypeStruct(shape, F32) for _, s...  247 us
    pallas_call x1, Pallas kernels, run_update(): pl.pallas_call(body, grid=(vr // step,), in_specs=[spec(norm.shape, True)...  8.45 us

profile of v6, /device:TPU:0, one launch (start us, length us, event | category | flops | bytes accessed | tf_op | source)
XLA Modules:
  0.0 256.5 jit_solution(5052151869515763255)
XLA Ops:
  0.7 247.2 %shard_map.456 = (f32[512,1024]{1,0:T(8,128)}, f32[512,1024]{1,0:T(8,128)}, f32[3,128,256]{2,1,0:T(8,128)}, f32[128,256]{1,0:T(8,128)}, f32[128,1024]{1,0:T(8,12...) custom-call(bf16[512,1024]{1,0:T(8,128)(2,1)} %refs_0_.1, s32[1,96]{1,0:T(1,128)} %refs_1_.1, ...), custom_call_target="tpu_custom_call" | custom-call | flops 20000000000 | bytes 20000000 | tf_op jit(solution)/shard_map/pallas_call | solution.py:1273
  247.8 8.5 %shard_map.457 = (f32[3,128,256]{2,1,0:T(8,128)}, f32[3,128,256]{2,1,0:T(8,128)}, f32[3,128,256]{2,1,0:T(8,128)}, f32[3,128,256]{2,1,0:T(8,128)}, bf16[3,128,256...) custom-call(f32[8,128]{1,0:T(8,128)} %get-tuple-element.64.refs_0_, ...), custom_call_target="tpu_custom_call" | custom-call | flops 7872000 | bytes 15744000 | tf_op jit(solution)/shard_map/pallas_call | solution.py:1345

commit v7 on v6

--- a/solution.py
+++ b/solution.py
@@ -113,6 +113,15 @@
             device_id=device,
             device_id_type=MESH,
         )
+
+    loads = [
+        pltpu.make_async_copy(source, target, r.lsem.at[k])
+        for k, (source, target) in enumerate(
+            ((r.expand, r.expand_in), (r.narrow, r.narrow_in), (r.tok, r.tok_in))
+        )
+    ]
+    for load in loads:
+        load.start()
 
     barrier = pltpu.get_barrier_semaphore()
 
@@ -416,8 +425,11 @@
     r.vb[2] = r.vb[0] + r.vb[1]
     swap_x = remote(r.vb.at[2], r.vb.at[3], r.vxs.at[1], r.vxr.at[1], x_peer)
     swap_x.start()
-    r.we[mine, :] = r.expand[...].astype(BF)
-    r.wn[mine, :] = r.narrow[...].astype(BF)
+    loads[0].wait()
+    r.we[mine, :] = r.expand_in[...].astype(BF)
+    loads[1].wait()
+    r.wn[mine, :] = r.narrow_in[...].astype(BF)
+    loads[2].wait()
     swap_x.wait_recv()
     r.wv[d] = r.vb[2] + r.vb[3]
     gather_start_y(VEC)
@@ -458,7 +470,7 @@
         hot = r.oht[where, :]
         keep = 1.0 - jnp.sum(hot.astype(F32), axis=1, keepdims=True)
         r.keep[where, :] = keep
-        r.xl[where, :] = (r.tok[where, :].astype(F32) * keep + nn(hot, r.slt[...])).astype(BF)
+        r.xl[where, :] = (r.tok_in[where, :].astype(F32) * keep + nn(hot, r.slt[...])).astype(BF)
 
     loop(rows // SUB, embed)
     r.st[...] = r.xl[aligned(own0, half), :].astype(F32)
@@ -1212,6 +1224,7 @@
         ("qc", (heads, SLOTS, LANES)),
         ("pc", (heads, rows, SLOTS)),
         ("cct", (hw, SLOTS)),
+        ("tok_in", (rows, d_model)),
     ]
     full = [
         ("vt", (16, d_model)),
@@ -1227,6 +1240,8 @@
         ("part", (SLOTS, TILE)),
         ("vf", (4, 16, vr)),
         ("vs", (16, vr)),
+        ("expand_in", (vr, uw)),
+        ("narrow_in", (vr, uw)),
         ("nm", (4, 8, LANES)),
         ("nz", (n, 8, LANES)),
     ]
@@ -1248,6 +1263,7 @@
         ("vxs", (4,)),
         ("vxr", (4,)),
         ("osem", (8,)),
+        ("lsem", (3,)),
         ("nms", (3,)),
         ("nmr", (3,)),
         ("nzs", (2, lines)),
@@ -1273,7 +1289,12 @@
     return pl.pallas_call(
         body,
         out_shape=[jax.ShapeDtypeStruct(shape, F32) for _, shape, _ in outputs],
-        in_specs=[pl.BlockSpec(memory_space=pltpu.VMEM)] * len(inputs),
+        in_specs=[
+            pl.BlockSpec(
+                memory_space=pl.ANY if name in ("tok", "expand", "narrow") else pltpu.VMEM
+            )
+            for name, _ in inputs
+        ],
         out_specs=[pl.BlockSpec(memory_space=space) for _, _, space in outputs],
         scratch_shapes=[pltpu.VMEM(shape, BF) for _, shape in low]
         + [pltpu.VMEM(shape, F32) for _, shape in full]

time: 257 us -> 256 us (level)
  no operation moved by 1% of the time
where the time goes in v7:
time: 256 us
  Pallas kernels  255 us (100%)
    pallas_call x1, Pallas kernels, run_layers(): pl.pallas_call(body, out_shape=[jax.ShapeDtypeStruct(shape, F32) for _, s...  247 us
    pallas_call x1, Pallas kernels, run_update(): pl.pallas_call(body, grid=(vr // step,), in_specs=[spec(norm.shape, True)...  8.45 us

profile of v7, /device:TPU:0, one launch (start us, length us, event | category | flops | bytes accessed | tf_op | source)
XLA Modules:
  0.0 255.9 jit_solution(11512800640688558103)
XLA Ops:
  0.7 246.6 %shard_map.456 = (f32[512,1024]{1,0:T(8,128)}, f32[512,1024]{1,0:T(8,128)}, f32[3,128,256]{2,1,0:T(8,128)}, f32[128,256]{1,0:T(8,128)}, f32[128,1024]{1,0:T(8,12...) custom-call(bf16[512,1024]{1,0:T(8,128)(2,1)} %refs_0_.1, s32[1,96]{1,0:T(1,128)} %refs_1_.1, ...), custom_call_target="tpu_custom_call" | custom-call | flops 20000000000 | bytes 20000000 | tf_op jit(solution)/shard_map/pallas_call | solution.py:1289
  247.3 8.5 %shard_map.457 = (f32[3,128,256]{2,1,0:T(8,128)}, f32[3,128,256]{2,1,0:T(8,128)}, f32[3,128,256]{2,1,0:T(8,128)}, f32[3,128,256]{2,1,0:T(8,128)}, bf16[3,128,256...) custom-call(f32[8,128]{1,0:T(8,128)} %get-tuple-element.64.refs_0_, ...), custom_call_target="tpu_custom_call" | custom-call | flops 7872000 | bytes 15744000 | tf_op jit(solution)/shard_map/pallas_call | solution.py:1366

commit v8 on v7

--- a/solution.py
+++ b/solution.py
@@ -289,7 +289,7 @@
 
     def scatter_next():
         while queue and queue[0][0] in ready:
-            if sum(weight_of[region] for region, _ in under_way) > 4:
+            if sum(weight_of[region] for region, _ in under_way) > 8:
                 break
             region, turn = queue.pop(0)
             scatter_y(region, scatter_order(turn)).start()

time: 256 us -> 256 us (level)
  no operation moved by 1% of the time
where the time goes in v8:
time: 256 us
  Pallas kernels  255 us (100%)
    pallas_call x1, Pallas kernels, run_layers(): pl.pallas_call(body, out_shape=[jax.ShapeDtypeStruct(shape, F32) for _, s...  247 us
    pallas_call x1, Pallas kernels, run_update(): pl.pallas_call(body, grid=(vr // step,), in_specs=[spec(norm.shape, True)...  8.45 us

profile of v8, /device:TPU:0, one launch (start us, length us, event | category | flops | bytes accessed | tf_op | source)
XLA Modules:
  0.0 255.9 jit_solution(14033539553238763234)
XLA Ops:
  0.7 246.6 %shard_map.456 = (f32[512,1024]{1,0:T(8,128)}, f32[512,1024]{1,0:T(8,128)}, f32[3,128,256]{2,1,0:T(8,128)}, f32[128,256]{1,0:T(8,128)}, f32[128,1024]{1,0:T(8,12...) custom-call(bf16[512,1024]{1,0:T(8,128)(2,1)} %refs_0_.1, s32[1,96]{1,0:T(1,128)} %refs_1_.1, ...), custom_call_target="tpu_custom_call" | custom-call | flops 20000000000 | bytes 20000000 | tf_op jit(solution)/shard_map/pallas_call | solution.py:1289
  247.3 8.5 %shard_map.457 = (f32[3,128,256]{2,1,0:T(8,128)}, f32[3,128,256]{2,1,0:T(8,128)}, f32[3,128,256]{2,1,0:T(8,128)}, f32[3,128,256]{2,1,0:T(8,128)}, bf16[3,128,256...) custom-call(f32[8,128]{1,0:T(8,128)} %get-tuple-element.64.refs_0_, ...), custom_call_target="tpu_custom_call" | custom-call | flops 7872000 | bytes 15744000 | tf_op jit(solution)/shard_map/pallas_call | solution.py:1366
